TPU v7x, 32 devices: a whole 2x2x4 slice. The times are simulated.
32 devices in a mesh: gx: 4 (over y, core), gy: 4 (over z), gz: 2 (over x).
Axes of the slice: x: 2, y: 2, z: 4, core: 2. Of those that a mesh axis runs over, the one named last changes fastest.
Arguments:
- tokens: bfloat16 [512, 8192], P('gx', ('gz', 'gy')), may hold values from -6 to 6
- gate_weight: bfloat16 [14336, 8192], P(('gy', 'gx'), 'gz'), may hold values from -0.0625 to 0.0625
- up_weight: bfloat16 [14336, 8192], P(('gy', 'gx'), 'gz'), may hold values from -0.0625 to 0.0625
- down_weight: bfloat16 [14336, 8192], P(('gy', 'gx'), 'gz'), may hold values from -0.046875 to 0.046875
- reward_head: bfloat16 [8192], P(('gz', 'gy')), may hold values from -0.0625 to 0.0625
- lm_grad: float32 [512, 8192], P('gx', ('gz', 'gy')), may hold values from -6 to 6
- pair_index: int32 [2, 2], replicated, may hold values from 0 to 3, as said below
Outputs:
- grad_tokens: float32 [512, 8192], P('gx', ('gz', 'gy'))
- grad_gate: float32 [14336, 8192], P(('gy', 'gx'), 'gz')
- grad_up: float32 [14336, 8192], P(('gy', 'gx'), 'gz')
- grad_down: float32 [14336, 8192], P(('gy', 'gx'), 'gz')
- rewards: float32 [4], replicated
Inputs may be any that keep to these rules, and one draw needn't show every extreme that they name: Every sequence number of 0 to 3 stands exactly once in pair_index.
All inputs are finite; a program needn't handle non-finite values.
Results may differ from a plain program's by a relative error of at most 0.008.
Values may be sent and summed in bfloat16 or wider, within the bound.
A program may use at most 256 MiB of HBM per device.

v0:
```python
import jax
import jax.numpy as jnp
from jax import lax
from jax.sharding import PartitionSpec as P

SEQ_LEN = 128


reward_weight = 64.0


def feature_blocks(shard):
    return lax.all_gather(shard, "gy", axis=1, tiled=True)


def output_sums(partial_value):
    return lax.psum_scatter(partial_value, "gy", scatter_dimension=1, tiled=True)


def right_product(left, right):
    return lax.dot_general(
        left, right, (((1,), (1,)), ((), ())), preferred_element_type=jnp.float32
    )


def body(tokens, gate_weight, up_weight, down_weight, reward_head, lm_grad, pair_index):
    row_count = tokens.shape[0]
    tok_block = feature_blocks(tokens)
    gate_full, up_full, down_full = (
        lax.all_gather(gate_weight, "gx", axis=0, tiled=True),
        lax.all_gather(up_weight, "gx", axis=0, tiled=True),
        lax.all_gather(down_weight, "gx", axis=0, tiled=True),
    )
    gate_part = right_product(tok_block, gate_full)
    up_part = right_product(tok_block, up_full)
    gate_sum, up_sum = (
        lax.psum_scatter(gate_part, "gz", scatter_dimension=1, tiled=True),
        lax.psum_scatter(up_part, "gz", scatter_dimension=1, tiled=True),
    )
    gate_sigmoid = jax.nn.sigmoid(gate_sum)
    silu_gate = gate_sum * gate_sigmoid
    hidden = (silu_gate * up_sum).astype(jnp.bfloat16)
    hidden_block = lax.all_gather(hidden, "gz", axis=1, tiled=True)
    ffn_out = output_sums(jnp.dot(hidden_block, down_full, preferred_element_type=jnp.float32))
    block_out = tokens.astype(jnp.float32) + ffn_out
    seq_dev = row_count // SEQ_LEN
    seq_total = seq_dev * lax.axis_size("gx")
    head_vec = reward_head.astype(jnp.float32)
    last_rows = block_out.reshape(seq_dev, SEQ_LEN, -1)[:, SEQ_LEN - 1, :]
    own_terms = jnp.sum(last_rows * head_vec[None, :], axis=1)
    offset = lax.axis_index("gx") * seq_dev
    spread = lax.dynamic_update_slice(jnp.zeros((seq_total,), jnp.float32), own_terms, (offset,))
    rewards = lax.psum(spread, ("gx", "gy", "gz"))
    sequence = jnp.arange(seq_total, dtype=jnp.int32)
    chosen_hot = (pair_index[:, 0:1] == sequence[None, :]).astype(jnp.float32)
    rejected_hot = (pair_index[:, 1:2] == sequence[None, :]).astype(jnp.float32)
    margin = jnp.sum(chosen_hot * rewards[None, :], axis=1) - jnp.sum(
        rejected_hot * rewards[None, :], axis=1
    )
    pair_weight = jax.nn.sigmoid(-margin)
    pair_coefs = jnp.sum((rejected_hot - chosen_hot) * pair_weight[:, None], axis=0)
    own_coefs = lax.dynamic_slice(pair_coefs, (offset,), (seq_dev,))
    head_term = reward_weight * own_coefs[:, None] * head_vec[None, :]
    grad_out = (
        lm_grad.reshape(seq_dev, SEQ_LEN, -1)
        .at[:, SEQ_LEN - 1, :]
        .add(head_term)
        .reshape(row_count, -1)
    )
    grad_low = grad_out.astype(jnp.bfloat16)
    grad_block = feature_blocks(grad_low)
    hidden_part = right_product(grad_block, down_full)
    hidden_grad = lax.psum_scatter(hidden_part, "gz", scatter_dimension=1, tiled=True)
    up_grad = (hidden_grad * silu_gate).astype(jnp.bfloat16)
    gate_grad = (
        hidden_grad * up_sum * gate_sigmoid * (1.0 + gate_sum * (1.0 - gate_sigmoid))
    ).astype(jnp.bfloat16)
    gate_grad_block, up_grad_block = (
        lax.all_gather(gate_grad, "gz", axis=1, tiled=True),
        lax.all_gather(up_grad, "gz", axis=1, tiled=True),
    )
    token_part = jnp.dot(gate_grad_block, gate_full, preferred_element_type=jnp.float32) + jnp.dot(
        up_grad_block, up_full, preferred_element_type=jnp.float32
    )
    grad_tokens = grad_out + output_sums(token_part)
    hidden_cols, gate_cols, up_cols = (
        lax.all_to_all(hidden_block, "gx", split_axis=1, concat_axis=0, tiled=True),
        lax.all_to_all(gate_grad_block, "gx", split_axis=1, concat_axis=0, tiled=True),
        lax.all_to_all(up_grad_block, "gx", split_axis=1, concat_axis=0, tiled=True),
    )
    tok_piece = lax.all_gather(tok_block, "gx", axis=0, tiled=True)
    grad_piece = lax.all_gather(grad_block, "gx", axis=0, tiled=True)
    gate_total = jnp.einsum("tf,td->fd", gate_cols, tok_piece, preferred_element_type=jnp.float32)
    up_total = jnp.einsum("tf,td->fd", up_cols, tok_piece, preferred_element_type=jnp.float32)
    down_total = jnp.einsum(
        "tf,td->fd", hidden_cols, grad_piece, preferred_element_type=jnp.float32
    )
    loss_scale = 1.0 / jnp.sqrt(jnp.float32(row_count * lax.axis_size("gx")))
    return (
        grad_tokens,
        gate_total * loss_scale,
        up_total * loss_scale,
        down_total * loss_scale,
        rewards,
    )


def solution(mesh):
    placed = (
        P("gx", ("gz", "gy")),
        P(("gy", "gx"), "gz"),
        P(("gy", "gx"), "gz"),
        P(("gy", "gx"), "gz"),
        P(("gz", "gy")),
        P("gx", ("gz", "gy")),
        P(),
    )
    return jax.shard_map(
        body,
        mesh=mesh,
        in_specs=placed,
        out_specs=(
            P("gx", ("gz", "gy")),
            P(("gy", "gx"), "gz"),
            P(("gy", "gx"), "gz"),
            P(("gy", "gx"), "gz"),
            P(),
        ),
        check_vma=False,
    )
```

profile of v0, /device:TPU:0, one launch (start us, length us, event | category | flops | bytes accessed | tf_op | source)
XLA Modules:
  0.0 962.6 jit_solution(5711581941582726386)
XLA Ops:
  9.8 30.4 %all-gather.8.cloned.1.call-done = bf16[128,4096]{1,0:T(8,128)(2,1)} async-done(((bf16[128,1024]{1,0:T(8,128)(2,1)}), bf16[128,4096]{1,0:T(8,128)(2,1)}) %all-gather.8.cloned.1.call-update) | async-done | bytes 1048592 | tf_op jit(solution)/shard_map/all_gather | solution.py:13
  40.2 179.1 %all-gather.10.cloned.1.call-done = bf16[3584,4096]{1,0:T(8,128)(2,1)} async-done(((bf16[896,4096]{1,0:T(8,128)(2,1)}), bf16[3584,4096]{1,0:T(8,128)(2,1)}) %all-gather.10.cloned.1.call-update) | async-done | bytes 29360144 | tf_op jit(solution)/shard_map/all_gather | solution.py:30
  219.3 17.4 %fusion.2 = f32[128,3584]{1,0:T(8,128)} fusion(bf16[128,4096]{1,0:T(8,128)(2,1)} %all-gather.8.cloned.1.call-done, bf16[3584,4096]{1,0:T(8,128)(2,1)} %all-gather.10.cloned.1.call-done), kind=kOutput, calls=%fused_computation.25 | convolution fusion | flops 3758096384 | bytes 32243712 | tf_op jit(solution)/shard_map/dot_general | solution.py:21
  236.9 162.1 %all-gather.12.cloned.1.call-done = bf16[3584,4096]{1,0:T(8,128)(2,1)} async-done(((bf16[896,4096]{1,0:T(8,128)(2,1)}), bf16[3584,4096]{1,0:T(8,128)(2,1)}) %all-gather.12.cloned.1.call-update) | async-done | bytes 29360144 | tf_op jit(solution)/shard_map/all_gather | solution.py:31
  399.0 16.3 %fusion.3 = f32[128,3584]{1,0:T(8,128)} fusion(bf16[128,4096]{1,0:T(8,128)(2,1)S(1)} %copy-done, bf16[3584,4096]{1,0:T(8,128)(2,1)} %all-gather.12.cloned.1.call-done), kind=kOutput, calls=%fused_computation.26 | convolution fusion | flops 3758096384 | bytes 32243712 | tf_op jit(solution)/shard_map/dot_general | solution.py:21
  415.9 14.7 %reduce-scatter.6.cloned.1.call-done = f32[128,1792]{1,0:T(8,128)} async-done(((f32[128,3584]{1,0:T(8,128)}), f32[128,1792]{1,0:T(8,128)}) %reduce-scatter.6.cloned.1.call-update) | async-done | bytes 917520 | tf_op jit(solution)/shard_map/reduce_scatter | solution.py:37
  430.6 31.7 %reduce-scatter.8.cloned.1.call-done = f32[128,1792]{1,0:T(8,128)} async-done(((f32[128,3584]{1,0:T(8,128)}), f32[128,1792]{1,0:T(8,128)}) %reduce-scatter.8.cloned.1.call-update) | async-done | bytes 917520 | tf_op jit(solution)/shard_map/reduce_scatter | solution.py:38
  464.1 12.9 %all_gather.33 = bf16[128,3584]{1,0:T(8,128)(2,1)S(1)} all-gather(bf16[128,1792]{1,0:T(8,128)(2,1)S(1)} %multiply_convert_fusion.2), channel_id=1, replica_groups=mesh['gx'=4,'gy'=4,'gz'=2] {'gz'}, dimensions={1}, use_global_device_ids=true | all-gather | bytes 1376256 | tf_op jit(solution)/shard_map/all_gather | solution.py:43
  477.0 164.8 %all-gather.14.cloned.1.call-done = bf16[3584,4096]{1,0:T(8,128)(2,1)} async-done(((bf16[896,4096]{1,0:T(8,128)(2,1)}), bf16[3584,4096]{1,0:T(8,128)(2,1)}) %all-gather.14.cloned.1.call-update) | async-done | bytes 29360144 | tf_op jit(solution)/shard_map/all_gather | solution.py:32
  641.8 12.9 %fusion.4 = f32[128,4096]{1,0:T(8,128)} fusion(bf16[128,3584]{1,0:T(8,128)(2,1)S(1)} %all_gather.33, bf16[3584,4096]{1,0:T(8,128)(2,1)} %all-gather.14.cloned.1.call-done), kind=kOutput, calls=%fused_computation.27 | convolution fusion | flops 3758096384 | bytes 32374784 | tf_op jit(solution)/shard_map/dot_general | solution.py:44
  655.0 43.8 %reduce-scatter.10.cloned.1.call-done = f32[128,1024]{1,0:T(8,128)} async-done(((f32[128,4096]{1,0:T(8,128)}), f32[128,1024]{1,0:T(8,128)}) %reduce-scatter.10.cloned.1.call-update) | async-done | bytes 524304 | tf_op jit(solution)/shard_map/reduce_scatter | solution.py:17
  701.3 39.5 %psum.7 = f32[4]{0:T(128)S(1)} all-reduce(f32[4]{0:T(128)S(1)} %dynamic_update_slice.3), channel_id=1, replica_groups=mesh['gx'=4,'gy'=4,'gz'=2] {'gx','gy','gz'}, use_global_device_ids=true, to_apply=%region_4.0 | all-reduce | flops 4 | bytes 32 | tf_op jit(solution)/shard_map/psum | solution.py:53
  743.5 27.6 %all-gather.16.cloned.1.call-done = bf16[128,4096]{1,0:T(8,128)(2,1)} async-done(((bf16[128,1024]{1,0:T(8,128)(2,1)}), bf16[128,4096]{1,0:T(8,128)(2,1)}) %all-gather.16.cloned.1.call-update) | async-done | bytes 1048592 | tf_op jit(solution)/shard_map/all_gather | solution.py:13
  771.2 16.4 %fusion.5 = f32[128,3584]{1,0:T(8,128)} fusion(bf16[128,4096]{1,0:T(8,128)(2,1)} %all-gather.16.cloned.1.call-done, bf16[3584,4096]{1,0:T(8,128)(2,1)} %all-gather.14.cloned.1.call-done), kind=kOutput, calls=%fused_computation.28 | convolution fusion | flops 3758096384 | bytes 32243712 | tf_op jit(solution)/shard_map/dot_general | solution.py:21
  788.9 27.3 %reduce-scatter.12.cloned.1.call-done = f32[128,1792]{1,0:T(8,128)} async-done(((f32[128,3584]{1,0:T(8,128)}), f32[128,1792]{1,0:T(8,128)}) %reduce-scatter.12.cloned.1.call-update) | async-done | bytes 917520 | tf_op jit(solution)/shard_map/reduce_scatter | solution.py:73
  818.6 12.9 %all_gather.37 = bf16[128,3584]{1,0:T(8,128)(2,1)S(1)} all-gather(bf16[128,1792]{1,0:T(8,128)(2,1)S(1)} %get-tuple-element.21), channel_id=1, replica_groups=mesh['gx'=4,'gy'=4,'gz'=2] {'gz'}, dimensions={1}, use_global_device_ids=true | all-gather | bytes 1376256 | tf_op jit(solution)/shard_map/all_gather | solution.py:80
  836.8 13.7 %all_gather.36 = bf16[128,3584]{1,0:T(8,128)(2,1)S(1)} all-gather(bf16[128,1792]{1,0:T(8,128)(2,1)} %get-tuple-element.22), channel_id=1, replica_groups=mesh['gx'=4,'gy'=4,'gz'=2] {'gz'}, dimensions={1}, use_global_device_ids=true | all-gather | bytes 1376256 | tf_op jit(solution)/shard_map/all_gather | solution.py:79
  850.5 11.5 %fusion.6 = f32[128,4096]{1,0:T(8,128)S(1)} fusion(bf16[128,3584]{1,0:T(8,128)(2,1)S(1)} %all_gather.36, bf16[3584,4096]{1,0:T(8,128)(2,1)} %all-gather.10.cloned.1.call-done), kind=kOutput, calls=%fused_computation.29 | convolution fusion | flops 3758096384 | bytes 32374784 | tf_op jit(solution)/shard_map/dot_general | solution.py:82
  862.0 15.4 %convolution_add_fusion = f32[128,4096]{1,0:T(8,128)} fusion(f32[128,4096]{1,0:T(8,128)S(1)} %fusion.6, bf16[128,3584]{1,0:T(8,128)(2,1)S(1)} %all_gather.37, bf16[3584,4096]{1,0:T(8,128)(2,1)} %all-gather.12.cloned.1.call-done), kind=kOutput, calls=%fused_computation.3 | convolution fusion | flops 3758620672 | bytes 34471936 | tf_op jit(solution)/shard_map/dot_general | solution.py:82
  883.3 12.0 %convolution_multiply_fusion.1 = f32[896,4096]{1,0:T(8,128)} fusion(bf16[512,896]{1,0:T(8,128)(2,1)} %bitcast.8, bf16[512,4096]{1,0:T(8,128)(2,1)} %all-gather.18.cloned.1.call-done), kind=kOutput, calls=%fused_computation.1 | convolution fusion | flops 3761766400 | bytes 19791872 | tf_op jit(solution)/shard_map/tf,td->fd/dot_general | solution.py:94
  895.2 10.9 %all-to-all-done = bf16[128,4,896]{2,0,1:T(8,128)(2,1)S(1)} async-done(((bf16[128,4,896]{2,0,1:T(8,128)(2,1)}), bf16[128,4,896]{2,0,1:T(8,128)(2,1)S(1)}, u32[]{:S(2)}, u32[]{:S(2)}) %all-to-all-start) | async-done | bytes 917536 | tf_op jit(solution)/shard_map/all_to_all | solution.py:88
  909.6 11.7 %convolution_multiply_fusion.2 = f32[896,4096]{1,0:T(8,128)} fusion(bf16[512,896]{1,0:T(8,128)(2,1)S(1)} %bitcast.48, bf16[512,4096]{1,0:T(8,128)(2,1)} %all-gather.18.cloned.1.call-done), kind=kOutput, calls=%fused_computation.2 | convolution fusion | flops 3761766400 | bytes 19791872 | tf_op jit(solution)/shard_map/tf,td->fd/dot_general | solution.py:93
  922.6 11.7 %convolution_multiply_fusion = f32[896,4096]{1,0:T(8,128)} fusion(bf16[512,896]{1,0:T(8,128)(2,1)S(1)} %bitcast.49, bf16[512,4096]{1,0:T(8,128)(2,1)} %all-gather.20.cloned.1.call-done), kind=kOutput, calls=%fused_computation | convolution fusion | flops 3761766400 | bytes 19791872 | tf_op jit(solution)/shard_map/tf,td->fd/dot_general | solution.py:95
  934.3 19.6 %reduce-scatter.14.cloned.1.call-done = f32[128,1024]{1,0:T(8,128)} async-done(((f32[128,4096]{1,0:T(8,128)}), f32[128,1024]{1,0:T(8,128)}) %reduce-scatter.14.cloned.1.call-update) | async-done | bytes 524304 | tf_op jit(solution)/shard_map/reduce_scatter | solution.py:17
  (66 shorter events, 31.3 us)
Async XLA Ops:
  7.2 33.1 %all-gather.8.cloned.1.call-start = ((), (), s32[]{:S(2)}) async-start(), calls=%async_computation.8 | async-start | bytes 1310720 | tf_op jit(solution)/shard_map/all_gather | solution.py:13
  8.3 211.1 %all-gather.10.cloned.1.call-start = ((), (), s32[]{:S(2)}) async-start(), calls=%async_computation.9 | async-start | bytes 36700160 | tf_op jit(solution)/shard_map/all_gather | solution.py:30
  9.0 389.9 %all-gather.12.cloned.1.call-start = ((), (), s32[]{:S(2)}) async-start(), calls=%async_computation.11 | async-start | bytes 36700160 | tf_op jit(solution)/shard_map/all_gather | solution.py:31
  9.8 420.9 %reduce-scatter.6.cloned.1.call-start = ((), (), s32[]{:S(2)}) async-start(), calls=%async_computation.10 | async-start | bytes 2752512 | tf_op jit(solution)/shard_map/reduce_scatter | solution.py:37
  40.2 358.7 %copy-start = (bf16[128,4096]{1,0:T(8,128)(2,1)S(1)}, bf16[128,4096]{1,0:T(8,128)(2,1)}, u32[]{:S(2)}) copy-start(bf16[128,4096]{1,0:T(8,128)(2,1)} %all-gather.8.cloned.1.call-done) | copy-start | bytes 3145732
  236.8 225.5 %reduce-scatter.8.cloned.1.call-start = ((), (), s32[]{:S(2)}) async-start(), calls=%async_computation.12 | async-start | bytes 2752512 | tf_op jit(solution)/shard_map/reduce_scatter | solution.py:38
  415.3 226.6 %all-gather.14.cloned.1.call-start = ((), (), s32[]{:S(2)}) async-start(), calls=%async_computation.13 | async-start | bytes 36700160 | tf_op jit(solution)/shard_map/all_gather | solution.py:32
  415.9 283.0 %reduce-scatter.10.cloned.1.call-start = ((), (), s32[]{:S(2)}) async-start(), calls=%async_computation.14 | async-start | bytes 2621440 | tf_op jit(solution)/shard_map/reduce_scatter | solution.py:17
  477.0 177.8 %copy-start.5 = (s32[2,2]{1,0:T(2,128)S(1)}, s32[2,2]{1,0:T(2,128)}, u32[]{:S(2)}) copy-start(s32[2,2]{1,0:T(2,128)} %param.15) | copy-start | bytes 52
  477.0 221.8 %copy-start.3 = (bf16[128,1024]{1,0:T(8,128)(2,1)S(1)}, bf16[128,1024]{1,0:T(8,128)(2,1)}, u32[]{:S(2)}) copy-start(bf16[128,1024]{1,0:T(8,128)(2,1)} %param.9) | copy-start | bytes 786436
  477.0 222.9 %copy-start.4 = (bf16[1024]{0:T(1024)(128)(2,1)S(1)}, bf16[1024]{0:T(1024)(128)(2,1)}, u32[]{:S(2)}) copy-start(bf16[1024]{0:T(1024)(128)(2,1)} %param.13) | copy-start | bytes 6148
  654.8 116.4 %all-gather.16.cloned.1.call-start = ((), (), s32[]{:S(2)}) async-start(), calls=%async_computation.15 | async-start | bytes 1310720 | tf_op jit(solution)/shard_map/all_gather | solution.py:13
  740.8 46.7 %copy-start.6 = (f32[4]{0:T(128)}, f32[4]{0:T(128)S(1)}, u32[]{:S(2)}) copy-start(f32[4]{0:T(128)S(1)} %psum.7) | copy-start | bytes 52
  743.3 72.9 %reduce-scatter.12.cloned.1.call-start = ((), (), s32[]{:S(2)}) async-start(), calls=%async_computation.16 | async-start | bytes 2752512 | tf_op jit(solution)/shard_map/reduce_scatter | solution.py:73
  771.2 45.0 %copy-start.1 = (f32[128,1792]{1,0:T(8,128)S(1)}, f32[128,1792]{1,0:T(8,128)}, u32[]{:S(2)}) copy-start(f32[128,1792]{1,0:T(8,128)} %reduce-scatter.6.cloned.1.call-done) | copy-start | bytes 2752516
  771.2 45.0 %copy-start.2 = (f32[128,1792]{1,0:T(8,128)S(1)}, f32[128,1792]{1,0:T(8,128)}, u32[]{:S(2)}) copy-start(f32[128,1792]{1,0:T(8,128)} %reduce-scatter.8.cloned.1.call-done) | copy-start | bytes 2752516
  787.6 95.7 %all-gather.18.cloned.1.call-start = ((), (), s32[]{:S(2)}) async-start(), calls=%async_computation.18 | async-start | bytes 5242880 | tf_op jit(solution)/shard_map/all_gather | solution.py:91
  788.2 134.5 %all-gather.20.cloned.1.call-start = ((), (), s32[]{:S(2)}) async-start(), calls=%async_computation.19 | async-start | bytes 5242880 | tf_op jit(solution)/shard_map/all_gather | solution.py:92
  832.5 47.0 %all-to-all-start.1 = ((bf16[128,4,896]{2,0,1:T(8,128)(2,1)}), bf16[128,4,896]{2,0,1:T(8,128)(2,1)}, u32[]{:S(2)}, u32[]{:S(2)}) async-start(bf16[128,4,896]{2,0,1:T(8,128)(2,1)} %bitcast.43), calls=%async_computation.6 | async-start | bytes 1835008 | tf_op jit(solution)/shard_map/all_to_all | solution.py:89
  836.7 117.1 %reduce-scatter.14.cloned.1.call-start = ((), (), s32[]{:S(2)}) async-start(), calls=%async_computation.17 | async-start | bytes 2621440 | tf_op jit(solution)/shard_map/reduce_scatter | solution.py:17
  879.5 26.6 %all-to-all-start = ((bf16[128,4,896]{2,0,1:T(8,128)(2,1)}), bf16[128,4,896]{2,0,1:T(8,128)(2,1)S(1)}, u32[]{:S(2)}, u32[]{:S(2)}) async-start(bf16[128,4,896]{2,0,1:T(8,128)(2,1)} %bitcast.44), calls=%async_computation.5 | async-start | bytes 1835008 | tf_op jit(solution)/shard_map/all_to_all | solution.py:88
  906.1 16.5 %all-to-all-start.2 = ((bf16[128,4,896]{2,0,1:T(8,128)(2,1)}), bf16[128,4,896]{2,0,1:T(8,128)(2,1)S(1)}, u32[]{:S(2)}, u32[]{:S(2)}) async-start(bf16[128,4,896]{2,0,1:T(8,128)(2,1)} %bitcast.42), calls=%async_computation.7 | async-start | bytes 1835008 | tf_op jit(solution)/shard_map/all_to_all | solution.py:87
Sparse Core Ops, SparseCore 0:
  9.6 30.6 all-gather.7
  41.8 177.4 all-gather.9
  220.9 177.9 all-gather.11
  401.6 28.9 reduce-scatter.5
  433.4 28.9 reduce-scatter.7
  463.8 178.0 all-gather.13
  654.9 43.8 reduce-scatter.9
  743.4 27.7 all-gather.15
  787.7 28.4 reduce-scatter.11
  817.6 44.2 all-gather.17
  863.5 44.3 all-gather.19
  910.0 43.8 reduce-scatter.13
where the time goes:
time: 963 us
  waiting for transfers between devices  717 us (74%)
  matrix products  125 us (13%)
  blocking collectives  79.1 us (8%)
  between operations  15 us (2%)
  starting transfers between devices  12.1 us (1%)
    all_gather x1, waiting for transfers between devices, body(): lax.all_gather(gate_weight, 'gx', axis=0, tiled=True)  179 us
    all_gather x1, waiting for transfers between devices, body(): lax.all_gather(down_weight, 'gx', axis=0, tiled=True)  165 us
    all_gather x1, waiting for transfers between devices, body(): lax.all_gather(up_weight, 'gx', axis=0, tiled=True)  162 us
    reduce_scatter x2, waiting for transfers between devices, output_sums(): lax.psum_scatter(partial_value, 'gy', scatter_dimension=1, tiled=True)  63.3 us
    all_gather x2, waiting for transfers between devices, feature_blocks(): return lax.all_gather(shard, 'gy', axis=1, tiled=True)  58.1 us
    dot_general x3, matrix products, right_product(): lax.dot_general(left, right, (((1,), (1,)), ((), ())), preferred_element_...  50.1 us
    psum x1, blocking collectives, body(): rewards = lax.psum(spread, ('gx', 'gy', 'gz'))  39.5 us
    reduce_scatter x1, waiting for transfers between devices, body(): lax.psum_scatter(up_part, 'gz', scatter_dimension=1, tiled=True)  31.7 us
  transfers between devices with their start and end apart: 15, of which 12 were waited for; matrix products, arithmetic and copies ran while one was open for 11% of the time, Pallas kernels for 0%

commit v1 on v0

v1 whole, which is shorter than its diff:
```python
import jax
import jax.numpy as jnp
from jax import lax
from jax.sharding import PartitionSpec as P

SEQ_LEN = 128


reward_weight = 64.0


def swap(value, axis, bit):
    size = lax.axis_size(axis)
    return lax.ppermute(value, axis, [(i, i ^ bit) for i in range(size)])


def bits_down(axis):
    bit = lax.axis_size(axis) // 2
    bits = []
    while bit >= 1:
        bits.append(bit)
        bit //= 2
    return bits


def gx_offsets():
    offsets = [0]
    for bit in bits_down("gx"):
        offsets = offsets + [offset ^ bit for offset in offsets]
    return offsets


def ordered_features(pieces):
    me = lax.axis_index("gy")
    stacked = jnp.stack(pieces)
    return jnp.concatenate(
        [lax.dynamic_index_in_dim(stacked, me ^ p, 0, keepdims=False) for p in range(len(pieces))],
        axis=-1,
    )


def gather_halves(shard):
    pieces = [[shard] + [swap(shard, "gy", j) for j in range(1, lax.axis_size("gy"))]]
    for bit in bits_down("gx")[:-1]:
        pieces = pieces + [[swap(piece, "gx", bit) for piece in row] for row in pieces]
    first = jnp.concatenate([ordered_features(row) for row in pieces], axis=0)
    return first, swap(first, "gx", 1)


def right_product(left, right):
    return lax.dot_general(
        left, right, (((1,), (1,)), ((), ())), preferred_element_type=jnp.float32
    )


def feature_sum(partial_value):
    size = lax.axis_size("gz")
    low = partial_value.astype(jnp.bfloat16)
    total = partial_value
    for j in range(1, size):
        total = total + swap(low, "gz", j).astype(jnp.float32)
    return total


def sum_all(value):
    for axis in ("gz", "gx", "gy"):
        for bit in bits_down(axis):
            value = value + swap(value, axis, bit)
    return value


def body(tokens, gate_weight, up_weight, down_weight, reward_head, lm_grad, pair_index):
    row_count, feature_count = tokens.shape
    seq_dev = row_count // SEQ_LEN
    gx_size = lax.axis_size("gx")
    gy_size = lax.axis_size("gy")
    seq_total = seq_dev * gx_size
    me = lax.axis_index("gx")
    offsets = gx_offsets()

    tok_halves = gather_halves(tokens)
    low_halves = gather_halves(lm_grad.astype(jnp.bfloat16))
    head_own = reward_head.astype(jnp.float32)
    head_block = ordered_features(
        [reward_head] + [swap(reward_head, "gy", j) for j in range(1, gy_size)]
    )
    head_wide = jnp.broadcast_to(head_block[None, :], (8, head_block.shape[0]))
    head_part = right_product(head_wide, down_weight)[0]
    head_sum = head_part
    for j in range(1, lax.axis_size("gz")):
        head_sum = head_sum + swap(head_part, "gz", j)

    gate_halves = [feature_sum(right_product(half, gate_weight)) for half in tok_halves]
    up_halves = [feature_sum(right_product(half, up_weight)) for half in tok_halves]
    base_halves = [feature_sum(right_product(half, down_weight)) for half in low_halves]

    gate_sum = jnp.concatenate(gate_halves, axis=0)
    up_sum = jnp.concatenate(up_halves, axis=0)
    hidden_base = jnp.concatenate(base_halves, axis=0)
    tok_all = jnp.concatenate(tok_halves, axis=0)
    low_all = jnp.concatenate(low_halves, axis=0)
    unit_count = gate_sum.shape[1]

    gate_sigmoid = jax.nn.sigmoid(gate_sum)
    silu_gate = gate_sum * gate_sigmoid
    hidden = (silu_gate * up_sum).astype(jnp.bfloat16)

    last_hidden = hidden.reshape(seq_total, SEQ_LEN, unit_count)[:, SEQ_LEN - 1, :]
    last_terms = jnp.sum(last_hidden.astype(jnp.float32) * head_part[None, :], axis=1)
    last_tokens = tokens.reshape(seq_dev, SEQ_LEN, feature_count)[:, SEQ_LEN - 1, :]
    own_terms = jnp.sum(last_tokens.astype(jnp.float32) * head_own[None, :], axis=1)
    place = (me ^ jnp.array(offsets, jnp.int32))[:, None] * seq_dev + jnp.arange(seq_dev)[None, :]
    place = place.reshape(-1)
    one_hot = (place[:, None] == jnp.arange(seq_total)[None, :]).astype(jnp.float32)
    local_terms = last_terms.at[:seq_dev].add(own_terms)
    rewards = sum_all(jnp.sum(one_hot * local_terms[:, None], axis=0))

    sequence = jnp.arange(seq_total, dtype=jnp.int32)
    chosen_hot = (pair_index[:, 0:1] == sequence[None, :]).astype(jnp.float32)
    rejected_hot = (pair_index[:, 1:2] == sequence[None, :]).astype(jnp.float32)
    margin = jnp.sum(chosen_hot * rewards[None, :], axis=1) - jnp.sum(
        rejected_hot * rewards[None, :], axis=1
    )
    pair_weight = jax.nn.sigmoid(-margin)
    pair_coefs = jnp.sum((rejected_hot - chosen_hot) * pair_weight[:, None], axis=0)
    coefs = reward_weight * jnp.sum(one_hot * pair_coefs[None, :], axis=1)

    def with_last(value, vector, scales):
        count = scales.shape[0]
        is_last = (jnp.arange(SEQ_LEN) == SEQ_LEN - 1).astype(jnp.float32)
        rows = (scales[:, None] * is_last[None, :]).reshape(count * SEQ_LEN)
        return value + rows[:, None] * vector[None, :]

    hidden_grad = with_last(hidden_base, head_sum, coefs)
    up_grad = (hidden_grad * silu_gate).astype(jnp.bfloat16)
    gate_grad = (
        hidden_grad * up_sum * gate_sigmoid * (1.0 + gate_sum * (1.0 - gate_sigmoid))
    ).astype(jnp.bfloat16)

    token_part = jnp.dot(gate_grad, gate_weight, preferred_element_type=jnp.float32) + jnp.dot(
        up_grad, up_weight, preferred_element_type=jnp.float32
    )
    for bit in reversed(bits_down("gx")):
        half = token_part.shape[0] // 2
        sent = token_part[half:].astype(jnp.bfloat16)
        token_part = token_part[:half] + swap(sent, "gx", bit).astype(jnp.float32)
    blocks = token_part.reshape(row_count, gy_size, feature_count)
    gy_me = lax.axis_index("gy")
    token_sum = lax.dynamic_index_in_dim(blocks, gy_me, 1, keepdims=False)
    for j in range(1, gy_size):
        sent = lax.dynamic_index_in_dim(blocks, gy_me ^ j, 1, keepdims=False)
        token_sum = token_sum + swap(sent.astype(jnp.bfloat16), "gy", j).astype(jnp.float32)
    grad_tokens = with_last(lm_grad, head_own, coefs[:seq_dev]) + token_sum

    grad_low = with_last(
        low_all.astype(jnp.float32), head_block.astype(jnp.float32), coefs
    ).astype(jnp.bfloat16)
    loss_scale = 1.0 / jnp.sqrt(jnp.float32(row_count * gx_size))

    def weight_grad(left, right):
        return jnp.einsum("tf,td->fd", left, right, preferred_element_type=jnp.float32) * loss_scale

    return (
        grad_tokens,
        weight_grad(gate_grad, tok_all),
        weight_grad(up_grad, tok_all),
        weight_grad(hidden, grad_low),
        rewards,
    )


def solution(mesh):
    placed = (
        P("gx", ("gz", "gy")),
        P(("gy", "gx"), "gz"),
        P(("gy", "gx"), "gz"),
        P(("gy", "gx"), "gz"),
        P(("gz", "gy")),
        P("gx", ("gz", "gy")),
        P(),
    )
    return jax.shard_map(
        body,
        mesh=mesh,
        in_specs=placed,
        out_specs=(
            P("gx", ("gz", "gy")),
            P(("gy", "gx"), "gz"),
            P(("gy", "gx"), "gz"),
            P(("gy", "gx"), "gz"),
            P(),
        ),
        check_vma=False,
    )
```

time: 963 us -> 266 us (0.28)
  waiting for transfers between devices: 717 us -> 80.2 us
  blocking collectives: 79.1 us -> 0 us
  matrix products: 125 us -> 81.5 us
  starting transfers between devices: 12.1 us -> 53.7 us
  other arithmetic: 8.76 us -> 36.5 us
  between operations: 15 us -> 1.86 us
    all_gather x7 -> x0, waiting for transfers between devices: 564 us -> none  [the longest x1 179 us: body(): lax.all_gather(gate_weight, 'gx', axis=0, tiled=True)]
    reduce_scatter x5 -> x0, waiting for transfers between devices: 137 us -> none  [the longest x2 63.3 us: output_sums(): lax.psum_scatter(partial_value, 'gy', scatter_dimension=1, tiled=True)]
    ppermute x0 -> x36, waiting for transfers between devices: none -> 80.2 us  [swap(): return lax.ppermute(value, axis, [(i, i ^ bit) for i in range(size)])]
    ppermute x0 -> x36, starting transfers between devices: none -> 53.7 us  [swap(): return lax.ppermute(value, axis, [(i, i ^ bit) for i in range(size)])]
    all_gather x3 -> x0, blocking collectives: 39.6 us -> none  [the longest x1 13.7 us: body(): lax.all_gather(gate_grad, 'gz', axis=1, tiled=True)]
    psum x1 -> x0, blocking collectives: 39.5 us -> none  [body(): rewards = lax.psum(spread, ('gx', 'gy', 'gz'))]
    concatenate x0 -> x4, other arithmetic: none -> 26.2 us  [the longest x2 26 us: gather_halves(): first = jnp.concatenate([ordered_features(row) for row in pieces], axis=0)]
    dot_general x6 -> x5, matrix products: 75.1 us -> 51.4 us  [the longest x3 34.3 us: weight_grad(): jnp.einsum('tf,td->fd', left, right, preferred_element_type=jnp.float32)]
  transfers between devices with their start and end apart: 15 -> 36, of which waited for: 12 -> 16; matrix products, arithmetic and copies ran while one was open for 11% -> 37% of each run, Pallas kernels for 0% -> 0%
where the time goes in v1:
time: 266 us; the launch traced here: 262 us
  matrix products  81.5 us (31%)
  waiting for transfers between devices  80.2 us (30%)
  starting transfers between devices  53.7 us (20%)
  other arithmetic  36.5 us (14%)
  local copies, waits for them, and re-layouts  8.17 us (3%)
    ppermute x36, waiting for transfers between devices, swap(): return lax.ppermute(value, axis, [(i, i ^ bit) for i in range(size)])  80.2 us
    ppermute x36, starting transfers between devices, swap(): return lax.ppermute(value, axis, [(i, i ^ bit) for i in range(size)])  53.7 us
    dot_general x3, matrix products, weight_grad(): jnp.einsum('tf,td->fd', left, right, preferred_element_type=jnp.float32)  34.3 us
    dot_general x7, matrix products, right_product(): lax.dot_general(left, right, (((1,), (1,)), ((), ())), preferred_element_...  30 us
    concatenate x2, other arithmetic, gather_halves(): first = jnp.concatenate([ordered_features(row) for row in pieces], axis=0)  26 us
    dot_general x1, matrix products, body(): jnp.dot(up_grad, up_weight, preferred_element_type=jnp.float32)  10.1 us
    dot_general x1, matrix products, body(): jnp.dot(gate_grad, gate_weight, preferred_element_type=jnp.float32)  7.03 us
  transfers between devices with their start and end apart: 36, of which 16 were waited for; matrix products, arithmetic and copies ran while one was open for 37% of the time, Pallas kernels for 0%

profile of v1, /device:TPU:0, one launch (start us, length us, event | category | flops | bytes accessed | tf_op | source)
XLA Modules:
  0.0 261.8 jit_solution(17869240409497286905)
XLA Ops:
  0.6 4.1 %collective-permute-start.13 = (bf16[1024]{0:T(1024)(128)(2,1)}, bf16[1024]{0:T(1024)(128)(2,1)S(1)}, u32[]{:S(2)}, u32[]{:S(2)}) collective-permute-start(bf16[1024]{0:T(1024)(128)(2,1)} %param.14), channel_id=1, source_target_pairs={{0,4},{2,6},{4,0},{6,2},{1,5},{3,7},{5,1},{7,3},{8,12},{10,14},{12... | collective-permute-start | bytes 6152 | tf_op jit(solution)/shard_map/ppermute | solution.py:14
  17.0 5.1 %convolution_reduce_fusion = f32[896]{0:T(1024)S(1)} fusion(bf16[1,4096]{1,0:T(2,128)(2,1)S(1)} %reshape.144, bf16[896,4096]{1,0:T(8,128)(2,1)} %param.13), kind=kOutput, calls=%fused_computation.39 | convolution fusion | flops 7340032 | bytes 7351808 | tf_op jit(solution)/shard_map/dot_general | solution.py:51
  27.4 11.0 %collective-permute-start.20 = (bf16[128,1024]{1,0:T(8,128)(2,1)S(1)}, bf16[128,1024]{1,0:T(8,128)(2,1)S(1)}, u32[]{:S(2)}, u32[]{:S(2)}) collective-permute-start(bf16[128,1024]{1,0:T(8,128)(2,1)S(1)} %convert_element_type.149), channel_id=1, source_target_pairs={{0,2},{2,0},{4,6},{6,4},{1,3},{3,1},{5,7},{7,5},{8,10},{10,8},{12,... | collective-permute-start | bytes 786440 | tf_op jit(solution)/shard_map/ppermute | solution.py:14
  39.0 6.1 %collective-permute-done.21 = bf16[128,1024]{1,0:T(8,128)(2,1)S(1)} collective-permute-done((bf16[128,1024]{1,0:T(8,128)(2,1)S(1)}, bf16[128,1024]{1,0:T(8,128)(2,1)S(1)}, u32[]{:S(2)}, u32[]{:S(2)}) %collective-permute-start.21) | collective-permute-done | bytes 262176 | tf_op jit(solution)/shard_map/ppermute | solution.py:14
  46.6 4.0 %collective-permute-done.1 = bf16[128,1024]{1,0:T(8,128)(2,1)S(1)} collective-permute-done((bf16[128,1024]{1,0:T(8,128)(2,1)}, bf16[128,1024]{1,0:T(8,128)(2,1)S(1)}, u32[]{:S(2)}, u32[]{:S(2)}) %collective-permute-start.1) | collective-permute-done | bytes 262176 | tf_op jit(solution)/shard_map/ppermute | solution.py:14
  61.5 4.1 %collective-permute-done.4 = bf16[128,1024]{1,0:T(8,128)(2,1)S(1)} collective-permute-done((bf16[128,1024]{1,0:T(8,128)(2,1)S(1)}, bf16[128,1024]{1,0:T(8,128)(2,1)S(1)}, u32[]{:S(2)}, u32[]{:S(2)}) %collective-permute-start.4) | collective-permute-done | bytes 262176 | tf_op jit(solution)/shard_map/ppermute | solution.py:14
  67.1 4.1 %collective-permute-done.6 = bf16[128,1024]{1,0:T(8,128)(2,1)S(1)} collective-permute-done((bf16[128,1024]{1,0:T(8,128)(2,1)S(1)}, bf16[128,1024]{1,0:T(8,128)(2,1)S(1)}, u32[]{:S(2)}, u32[]{:S(2)}) %collective-permute-start.6) | collective-permute-done | bytes 262176 | tf_op jit(solution)/shard_map/ppermute | solution.py:14
  71.6 12.8 %maximum_maximum_fusion = bf16[256,4096]{1,0:T(8,128)(2,1)S(1)} fusion(bf16[128,1024]{1,0:T(8,128)(2,1)S(1)} %get-tuple-element.33, bf16[128,1024]{1,0:T(8,128)(2,1)S(1)} %get-tuple-element.34, bf16[128,1024]{1,0:T(8,128)(2,1)S(1)} %get-tuple-element.35, bf16[128,1024]{1,0:T(8,128)(2,1)S(1)} %get-tuple-element.32, ...), kind=kLoop, calls=%fused_computation.29 | loop fusion | flops 16777216 | bytes 4194304 | tf_op jit(solution)/shard_map/concatenate | solution.py:46
  87.0 5.8 %fusion.40 = (bf16[256,896]{1,0:T(8,128)(2,1)S(1)}, f32[256,896]{1,0:T(8,128)S(1)}) fusion(bf16[256,4096]{1,0:T(8,128)(2,1)S(1)} %maximum_maximum_fusion, bf16[896,4096]{1,0:T(8,128)(2,1)} %param.12), kind=kOutput, calls=%fused_computation.122 | convolution fusion | flops 1879277568 | bytes 10813440 | tf_op jit(solution)/shard_map/dot_general | solution.py:51
  95.3 13.2 %maximum_maximum_fusion.1 = bf16[256,4096]{1,0:T(8,128)(2,1)S(1)} fusion(bf16[128,1024]{1,0:T(8,128)(2,1)S(1)} %get-tuple-element.41, bf16[128,1024]{1,0:T(8,128)(2,1)S(1)} %get-tuple-element.42, bf16[128,1024]{1,0:T(8,128)(2,1)S(1)} %get-tuple-element.43, bf16[128,1024]{1,0:T(8,128)(2,1)S(1)} %get-tuple-element.40, ...), kind=kLoop, calls=%fused_computation.30 | loop fusion | flops 16777216 | bytes 4194304 | tf_op jit(solution)/shard_map/concatenate | solution.py:46
  116.1 9.3 %collective-permute-done.27 = bf16[256,896]{1,0:T(8,128)(2,1)S(1)} collective-permute-done((bf16[256,896]{1,0:T(8,128)(2,1)S(1)}, bf16[256,896]{1,0:T(8,128)(2,1)S(1)}, u32[]{:S(2)}, u32[]{:S(2)}) %collective-permute-start.27) | collective-permute-done | bytes 458784 | tf_op jit(solution)/shard_map/ppermute | solution.py:14
  125.5 4.1 %fusion.41 = (bf16[256,896]{1,0:T(8,128)(2,1)S(1)}, f32[256,896]{1,0:T(8,128)S(1)}) fusion(bf16[256,4096]{1,0:T(8,128)(2,1)} %collective-permute-done.8, bf16[896,4096]{1,0:T(8,128)(2,1)S(1)} %bitcast.123), kind=kOutput, calls=%fused_computation.123 | convolution fusion | flops 1879277568 | bytes 10813440 | tf_op jit(solution)/shard_map/dot_general | solution.py:51
  131.2 6.1 %fusion.39 = (bf16[256,896]{1,0:T(8,128)(2,1)S(1)}, f32[256,896]{1,0:T(8,128)S(1)}) fusion(bf16[256,4096]{1,0:T(8,128)(2,1)} %collective-permute-done.8, bf16[896,4096]{1,0:T(8,128)(2,1)} %param.12), kind=kOutput, calls=%fused_computation.121 | convolution fusion | flops 1879277568 | bytes 10813440 | tf_op jit(solution)/shard_map/dot_general | solution.py:51
  137.9 4.0 %fusion.37 = (bf16[256,896]{1,0:T(8,128)(2,1)S(1)}, f32[256,896]{1,0:T(8,128)S(1)}) fusion(bf16[256,4096]{1,0:T(8,128)(2,1)} %collective-permute-done.28, bf16[896,4096]{1,0:T(8,128)(2,1)S(1)} %bitcast.99), kind=kOutput, calls=%fused_computation.119 | convolution fusion | flops 1879277568 | bytes 10813440 | tf_op jit(solution)/shard_map/dot_general | solution.py:51
  143.8 9.2 %collective-permute-done.11 = bf16[256,896]{1,0:T(8,128)(2,1)S(1)} collective-permute-done((bf16[256,896]{1,0:T(8,128)(2,1)S(1)}, bf16[256,896]{1,0:T(8,128)(2,1)S(1)}, u32[]{:S(2)}, u32[]{:S(2)}) %collective-permute-start.11) | collective-permute-done | bytes 458784 | tf_op jit(solution)/shard_map/ppermute | solution.py:14
  155.6 5.9 %collective-permute-done.29 = bf16[256,896]{1,0:T(8,128)(2,1)S(1)} collective-permute-done((bf16[256,896]{1,0:T(8,128)(2,1)S(1)}, bf16[256,896]{1,0:T(8,128)(2,1)S(1)}, u32[]{:S(2)}, u32[]{:S(2)}) %collective-permute-start.29) | collective-permute-done | bytes 458784 | tf_op jit(solution)/shard_map/ppermute | solution.py:14
  166.3 4.4 %collective-permute-done.18 = f32[4]{0:T(128)S(1)} collective-permute-done((f32[4]{0:T(128)S(1)}, f32[4]{0:T(128)S(1)}, u32[]{:S(2)}, u32[]{:S(2)}) %collective-permute-start.18) | collective-permute-done | bytes 48 | tf_op jit(solution)/shard_map/ppermute | solution.py:14
  175.7 7.0 %fusion.43 = f32[512,4096]{1,0:T(8,128)} fusion(bf16[512,896]{1,0:T(8,128)(2,1)S(1)} %multiply_convert_fusion.2, bf16[896,4096]{1,0:T(8,128)(2,1)S(1)} %bitcast.123), kind=kOutput, calls=%fused_computation.125 | convolution fusion | flops 3758096384 | bytes 16646144 | tf_op jit(solution)/shard_map/dot_general | solution.py:140
  182.8 10.1 %convolution_add_fusion = f32[512,4096]{1,0:T(8,128)S(1)} fusion(f32[512,4096]{1,0:T(8,128)} %fusion.43, bf16[896,4096]{1,0:T(8,128)(2,1)} %param.12, f32[256,896]{1,0:T(8,128)S(1)} %convert_add_fusion, f32[256,896]{1,0:T(8,128)S(1)} %convert_add_fusion.1, f32[896]{0:T(1024)S(1)} %add.143, f32[512]{0:T(512)S(1)} %multiply_bitcast_fusion, ...), kind=kOutput, calls=%fused_computation.4 | convolution fusion | flops 3764781056 | bytes 27792896 | tf_op jit(solution)/shard_map/dot_general | solution.py:140
  194.0 10.5 %convolution_multiply_fusion = f32[896,4096]{1,0:T(8,128)} fusion(bf16[256,4096]{1,0:T(8,128)(2,1)} %collective-permute-done.28, bf16[128,1024]{1,0:T(8,128)(2,1)S(1)} %copy-done.23, bf16[128,1024]{1,0:T(8,128)(2,1)S(1)} %copy-done.25, bf16[128,1024]{1,0:T(8,128)(2,1)S(1)} %copy-done.27, bf16[128,1024]{1,0:T(8,128)(2,1)S(1)} %copy-done.21, ...), kind=kOutput, calls=%fused_computation.1 | convolution fusion | flops 3809476608 | bytes 22562816 | tf_op jit(solution)/shard_map/tf,td->fd/dot_general | solution.py:161
  207.0 10.2 %convolution_multiply_fusion.1 = f32[896,4096]{1,0:T(8,128)} fusion(f32[256,896]{1,0:T(8,128)S(1)} %convert_add_fusion, f32[256,896]{1,0:T(8,128)S(1)} %convert_add_fusion.1, f32[896]{0:T(1024)S(1)} %add.143, f32[512]{0:T(512)S(1)} %multiply_bitcast_fusion, f32[256,896]{1,0:T(8,128)S(1)} %convert_add_fusion.4, f32[256,896]{1,0:T(8,128)S(1)} %convert_add_fusion.5, ...), kind=kOutput, calls=%fused_computation.2 | convolution fusion | flops 3804102656 | bytes 22550016 | tf_op jit(solution)/shard_map/tf,td->fd/dot_general | solution.py:161
  217.2 13.1 %collective-permute-done.32 = bf16[128,4096]{1,0:T(8,128)(2,1)S(1)} collective-permute-done((bf16[128,4096]{1,0:T(8,128)(2,1)S(1)}, bf16[128,4096]{1,0:T(8,128)(2,1)S(1)}, u32[]{:S(2)}, u32[]{:S(2)}) %collective-permute-start.32) | collective-permute-done | bytes 1048608 | tf_op jit(solution)/shard_map/ppermute | solution.py:14
  241.4 13.5 %convolution_multiply_fusion.2 = f32[896,4096]{1,0:T(8,128)} fusion(bf16[512,896]{1,0:T(8,128)(2,1)S(1)} %copy-done.33, bf16[256,4096]{1,0:T(8,128)(2,1)} %collective-permute-done.8, bf16[128,1024]{1,0:T(8,128)(2,1)S(1)} %copy-done.6, bf16[128,1024]{1,0:T(8,128)(2,1)S(1)} %copy-done.9, bf16[128,1024]{1,0:T(8,128)(2,1)S(1)} %copy-done.11, ...), kind=kOutput, calls=%fused_computation.3 | convolution fusion | flops 3799515136 | bytes 19791872 | tf_op jit(solution)/shard_map/tf,td->fd/dot_general | solution.py:161
  255.5 5.0 %collective-permute-done.34 = bf16[128,1024]{1,0:T(8,128)(2,1)S(1)} collective-permute-done((bf16[128,1024]{1,0:T(8,128)(2,1)S(1)}, bf16[128,1024]{1,0:T(8,128)(2,1)S(1)}, u32[]{:S(2)}, u32[]{:S(2)}) %collective-permute-start.34) | collective-permute-done | bytes 262176 | tf_op jit(solution)/shard_map/ppermute | solution.py:14
  (210 shorter events, 77.3 us)
Async XLA Ops:
  7.4 20.0 %collective-permute-start.22 = (bf16[128,1024]{1,0:T(8,128)(2,1)S(1)}, bf16[128,1024]{1,0:T(8,128)(2,1)S(1)}, u32[]{:S(2)}, u32[]{:S(2)}) collective-permute-start(bf16[128,1024]{1,0:T(8,128)(2,1)S(1)} %convert_element_type.149), channel_id=1, source_target_pairs={{0,6},{2,4},{4,2},{6,0},{1,7},{3,5},{5,3},{7,1},{8,14},{10,12},{12... | collective-permute-start | bytes 786440 | tf_op jit(solution)/shard_map/ppermute | solution.py:14
  11.3 33.8 %collective-permute-start.21 = (bf16[128,1024]{1,0:T(8,128)(2,1)S(1)}, bf16[128,1024]{1,0:T(8,128)(2,1)S(1)}, u32[]{:S(2)}, u32[]{:S(2)}) collective-permute-start(bf16[128,1024]{1,0:T(8,128)(2,1)S(1)} %convert_element_type.149), channel_id=1, source_target_pairs={{0,4},{2,6},{4,0},{6,2},{1,5},{3,7},{5,1},{7,3},{8,12},{10,14},{12... | collective-permute-start | bytes 786440 | tf_op jit(solution)/shard_map/ppermute | solution.py:14
  13.8 36.9 %collective-permute-start.1 = (bf16[128,1024]{1,0:T(8,128)(2,1)}, bf16[128,1024]{1,0:T(8,128)(2,1)S(1)}, u32[]{:S(2)}, u32[]{:S(2)}) collective-permute-start(bf16[128,1024]{1,0:T(8,128)(2,1)} %param.10), channel_id=1, source_target_pairs={{0,4},{2,6},{4,0},{6,2},{1,5},{3,7},{5,1},{7,3},{8,12},{10,14},{12... | collective-permute-start | bytes 786440 | tf_op jit(solution)/shard_map/ppermute | solution.py:14
  16.8 35.5 %collective-permute-start = (bf16[128,1024]{1,0:T(8,128)(2,1)}, bf16[128,1024]{1,0:T(8,128)(2,1)S(1)}, u32[]{:S(2)}, u32[]{:S(2)}) collective-permute-start(bf16[128,1024]{1,0:T(8,128)(2,1)} %param.10), channel_id=1, source_target_pairs={{0,2},{2,0},{4,6},{6,4},{1,3},{3,1},{5,7},{7,5},{8,10},{10,8},{12,... | collective-permute-start | bytes 786440 | tf_op jit(solution)/shard_map/ppermute | solution.py:14
  25.8 26.9 %collective-permute-start.2 = (bf16[128,1024]{1,0:T(8,128)(2,1)S(1)}, bf16[128,1024]{1,0:T(8,128)(2,1)S(1)}, u32[]{:S(2)}, u32[]{:S(2)}) collective-permute-start(bf16[128,1024]{1,0:T(8,128)(2,1)S(1)} %copy-done.34), channel_id=1, source_target_pairs={{0,6},{2,4},{4,2},{6,0},{1,7},{3,5},{5,3},{7,1},{8,14},{10,12},{12... | collective-permute-start | bytes 786440 | tf_op jit(solution)/shard_map/ppermute | solution.py:14
  27.4 26.9 %collective-permute-start.20 = (bf16[128,1024]{1,0:T(8,128)(2,1)S(1)}, bf16[128,1024]{1,0:T(8,128)(2,1)S(1)}, u32[]{:S(2)}, u32[]{:S(2)}) collective-permute-start(bf16[128,1024]{1,0:T(8,128)(2,1)S(1)} %convert_element_type.149), channel_id=1, source_target_pairs={{0,2},{2,0},{4,6},{6,4},{1,3},{3,1},{5,7},{7,5},{8,10},{10,8},{12,... | collective-permute-start | bytes 786440 | tf_op jit(solution)/shard_map/ppermute | solution.py:14
  52.2 13.3 %collective-permute-start.4 = (bf16[128,1024]{1,0:T(8,128)(2,1)S(1)}, bf16[128,1024]{1,0:T(8,128)(2,1)S(1)}, u32[]{:S(2)}, u32[]{:S(2)}) collective-permute-start(bf16[128,1024]{1,0:T(8,128)(2,1)S(1)} %collective-permute-done), channel_id=1, source_target_pairs={{0,16},{8,24},{16,0},{24,8},{1,17},{9,25},{17,1},{25,9},{2,18},{10... | collective-permute-start | bytes 786440 | tf_op jit(solution)/shard_map/ppermute | solution.py:14
  52.7 18.4 %collective-permute-start.6 = (bf16[128,1024]{1,0:T(8,128)(2,1)S(1)}, bf16[128,1024]{1,0:T(8,128)(2,1)S(1)}, u32[]{:S(2)}, u32[]{:S(2)}) collective-permute-start(bf16[128,1024]{1,0:T(8,128)(2,1)S(1)} %collective-permute-done.2), channel_id=1, source_target_pairs={{0,16},{8,24},{16,0},{24,8},{1,17},{9,25},{17,1},{25,9},{2,18},{10... | collective-permute-start | bytes 786440 | tf_op jit(solution)/shard_map/ppermute | solution.py:14
  54.4 38.4 %collective-permute-start.23 = (bf16[128,1024]{1,0:T(8,128)(2,1)S(1)}, bf16[128,1024]{1,0:T(8,128)(2,1)S(1)}, u32[]{:S(2)}, u32[]{:S(2)}) collective-permute-start(bf16[128,1024]{1,0:T(8,128)(2,1)S(1)} %convert_element_type.149), channel_id=1, source_target_pairs={{0,16},{8,24},{16,0},{24,8},{1,17},{9,25},{17,1},{25,9},{2,18},{10... | collective-permute-start | bytes 786440 | tf_op jit(solution)/shard_map/ppermute | solution.py:14
  55.1 39.3 %collective-permute-start.26 = (bf16[128,1024]{1,0:T(8,128)(2,1)S(1)}, bf16[128,1024]{1,0:T(8,128)(2,1)S(1)}, u32[]{:S(2)}, u32[]{:S(2)}) collective-permute-start(bf16[128,1024]{1,0:T(8,128)(2,1)S(1)} %collective-permute-done.22), channel_id=1, source_target_pairs={{0,16},{8,24},{16,0},{24,8},{1,17},{9,25},{17,1},{25,9},{2,18},{10... | collective-permute-start | bytes 786440 | tf_op jit(solution)/shard_map/ppermute | solution.py:14
  59.9 35.0 %collective-permute-start.25 = (bf16[128,1024]{1,0:T(8,128)(2,1)S(1)}, bf16[128,1024]{1,0:T(8,128)(2,1)S(1)}, u32[]{:S(2)}, u32[]{:S(2)}) collective-permute-start(bf16[128,1024]{1,0:T(8,128)(2,1)S(1)} %collective-permute-done.21), channel_id=1, source_target_pairs={{0,16},{8,24},{16,0},{24,8},{1,17},{9,25},{17,1},{25,9},{2,18},{10... | collective-permute-start | bytes 786440 | tf_op jit(solution)/shard_map/ppermute | solution.py:14
  65.6 29.4 %collective-permute-start.24 = (bf16[128,1024]{1,0:T(8,128)(2,1)S(1)}, bf16[128,1024]{1,0:T(8,128)(2,1)S(1)}, u32[]{:S(2)}, u32[]{:S(2)}) collective-permute-start(bf16[128,1024]{1,0:T(8,128)(2,1)S(1)} %collective-permute-done.20), channel_id=1, source_target_pairs={{0,16},{8,24},{16,0},{24,8},{1,17},{9,25},{17,1},{25,9},{2,18},{10... | collective-permute-start | bytes 786440 | tf_op jit(solution)/shard_map/ppermute | solution.py:14
  84.5 41.1 %collective-permute-start.8 = (bf16[256,4096]{1,0:T(8,128)(2,1)S(1)}, bf16[256,4096]{1,0:T(8,128)(2,1)}, u32[]{:S(2)}, u32[]{:S(2)}) collective-permute-start(bf16[256,4096]{1,0:T(8,128)(2,1)S(1)} %maximum_maximum_fusion), channel_id=1, source_target_pairs={{0,8},{8,0},{16,24},{24,16},{1,9},{9,1},{17,25},{25,17},{2,10},{10... | collective-permute-start | bytes 6291464 | tf_op jit(solution)/shard_map/ppermute | solution.py:14
  92.8 20.1 %collective-permute-start.7 = (bf16[256,896]{1,0:T(8,128)(2,1)S(1)}, bf16[256,896]{1,0:T(8,128)(2,1)S(1)}, u32[]{:S(2)}, u32[]{:S(2)}) collective-permute-start(bf16[256,896]{1,0:T(8,128)(2,1)S(1)} %get-tuple-element.56), channel_id=1, source_target_pairs={{0,1},{1,0},{2,3},{3,2},{4,5},{5,4},{6,7},{7,6},{8,9},{9,8},{10,11... | collective-permute-start | bytes 1376264 | tf_op jit(solution)/shard_map/ppermute | solution.py:14
  94.4 21.7 %collective-permute-start.10 = (bf16[256,896]{1,0:T(8,128)(2,1)S(1)}, bf16[256,896]{1,0:T(8,128)(2,1)S(1)}, u32[]{:S(2)}, u32[]{:S(2)}) collective-permute-start(bf16[256,896]{1,0:T(8,128)(2,1)S(1)} %get-tuple-element.52), channel_id=1, source_target_pairs={{0,1},{1,0},{2,3},{3,2},{4,5},{5,4},{6,7},{7,6},{8,9},{9,8},{10,11... | collective-permute-start | bytes 1376264 | tf_op jit(solution)/shard_map/ppermute | solution.py:14
  111.3 26.6 %collective-permute-start.28 = (bf16[256,4096]{1,0:T(8,128)(2,1)S(1)}, bf16[256,4096]{1,0:T(8,128)(2,1)}, u32[]{:S(2)}, u32[]{:S(2)}) collective-permute-start(bf16[256,4096]{1,0:T(8,128)(2,1)S(1)} %maximum_maximum_fusion.1), channel_id=1, source_target_pairs={{0,8},{8,0},{16,24},{24,16},{1,9},{9,1},{17,25},{25,17},{2,10},{10... | collective-permute-start | bytes 6291464 | tf_op jit(solution)/shard_map/ppermute | solution.py:14
  111.3 14.1 %collective-permute-start.27 = (bf16[256,896]{1,0:T(8,128)(2,1)S(1)}, bf16[256,896]{1,0:T(8,128)(2,1)S(1)}, u32[]{:S(2)}, u32[]{:S(2)}) collective-permute-start(bf16[256,896]{1,0:T(8,128)(2,1)S(1)} %get-tuple-element.48), channel_id=1, source_target_pairs={{0,1},{1,0},{2,3},{3,2},{4,5},{5,4},{6,7},{7,6},{8,9},{9,8},{10,11... | collective-permute-start | bytes 1376264 | tf_op jit(solution)/shard_map/ppermute | solution.py:14
  129.6 13.8 %collective-permute-start.9 = (bf16[256,896]{1,0:T(8,128)(2,1)S(1)}, bf16[256,896]{1,0:T(8,128)(2,1)S(1)}, u32[]{:S(2)}, u32[]{:S(2)}) collective-permute-start(bf16[256,896]{1,0:T(8,128)(2,1)S(1)} %get-tuple-element.54), channel_id=1, source_target_pairs={{0,1},{1,0},{2,3},{3,2},{4,5},{5,4},{6,7},{7,6},{8,9},{9,8},{10,11... | collective-permute-start | bytes 1376264 | tf_op jit(solution)/shard_map/ppermute | solution.py:14
  137.3 15.7 %collective-permute-start.11 = (bf16[256,896]{1,0:T(8,128)(2,1)S(1)}, bf16[256,896]{1,0:T(8,128)(2,1)S(1)}, u32[]{:S(2)}, u32[]{:S(2)}) collective-permute-start(bf16[256,896]{1,0:T(8,128)(2,1)S(1)} %get-tuple-element.50), channel_id=1, source_target_pairs={{0,1},{1,0},{2,3},{3,2},{4,5},{5,4},{6,7},{7,6},{8,9},{9,8},{10,11... | collective-permute-start | bytes 1376264 | tf_op jit(solution)/shard_map/ppermute | solution.py:14
  141.9 19.6 %collective-permute-start.29 = (bf16[256,896]{1,0:T(8,128)(2,1)S(1)}, bf16[256,896]{1,0:T(8,128)(2,1)S(1)}, u32[]{:S(2)}, u32[]{:S(2)}) collective-permute-start(bf16[256,896]{1,0:T(8,128)(2,1)S(1)} %get-tuple-element.46), channel_id=1, source_target_pairs={{0,1},{1,0},{2,3},{3,2},{4,5},{5,4},{6,7},{7,6},{8,9},{9,8},{10,11... | collective-permute-start | bytes 1376264 | tf_op jit(solution)/shard_map/ppermute | solution.py:14
  205.4 24.9 %collective-permute-start.32 = (bf16[128,4096]{1,0:T(8,128)(2,1)S(1)}, bf16[128,4096]{1,0:T(8,128)(2,1)S(1)}, u32[]{:S(2)}, u32[]{:S(2)}) collective-permute-start(bf16[128,4096]{1,0:T(8,128)(2,1)S(1)} %slice.89), channel_id=1, source_target_pairs={{0,16},{8,24},{16,0},{24,8},{1,17},{9,25},{17,1},{25,9},{2,18},{10... | collective-permute-start | bytes 3145736 | tf_op jit(solution)/shard_map/ppermute | solution.py:14
  236.9 18.6 %collective-permute-start.35 = (bf16[128,1024]{1,0:T(8,128)(2,1)S(1)}, bf16[128,1024]{1,0:T(8,128)(2,1)S(1)}, u32[]{:S(2)}, u32[]{:S(2)}) collective-permute-start(bf16[128,1024]{1,0:T(8,128)(2,1)S(1)} %bitcast.105), channel_id=1, source_target_pairs={{0,6},{2,4},{4,2},{6,0},{1,7},{3,5},{5,3},{7,1},{8,14},{10,12},{12... | collective-permute-start | bytes 786440 | tf_op jit(solution)/shard_map/ppermute | solution.py:14
  239.5 21.0 %collective-permute-start.34 = (bf16[128,1024]{1,0:T(8,128)(2,1)S(1)}, bf16[128,1024]{1,0:T(8,128)(2,1)S(1)}, u32[]{:S(2)}, u32[]{:S(2)}) collective-permute-start(bf16[128,1024]{1,0:T(8,128)(2,1)S(1)} %bitcast.104), channel_id=1, source_target_pairs={{0,4},{2,6},{4,0},{6,2},{1,5},{3,7},{5,1},{7,3},{8,12},{10,14},{12... | collective-permute-start | bytes 786440 | tf_op jit(solution)/shard_map/ppermute | solution.py:14
  239.5 21.0 %collective-permute-start.33 = (bf16[128,1024]{1,0:T(8,128)(2,1)S(1)}, bf16[128,1024]{1,0:T(8,128)(2,1)S(1)}, u32[]{:S(2)}, u32[]{:S(2)}) collective-permute-start(bf16[128,1024]{1,0:T(8,128)(2,1)S(1)} %bitcast.103), channel_id=1, source_target_pairs={{0,2},{2,0},{4,6},{6,4},{1,3},{3,1},{5,7},{7,5},{8,10},{10,8},{12,... | collective-permute-start | bytes 786440 | tf_op jit(solution)/shard_map/ppermute | solution.py:14
  (55 other events, 616.2 us)

commit v2 on v1

--- a/solution.py
+++ b/solution.py
@@ -1,6 +1,8 @@
 import jax
 import jax.numpy as jnp
 from jax import lax
+from jax.experimental import pallas as pl
+from jax.experimental.pallas import tpu as pltpu
 from jax.sharding import PartitionSpec as P
 
 SEQ_LEN = 128
@@ -69,7 +71,7 @@
     return value
 
 
-def body(tokens, gate_weight, up_weight, down_weight, reward_head, lm_grad, pair_index):
+def permute_body(tokens, gate_weight, up_weight, down_weight, reward_head, lm_grad, pair_index):
     row_count, feature_count = tokens.shape
     seq_dev = row_count // SEQ_LEN
     gx_size = lax.axis_size("gx")
@@ -167,6 +169,394 @@
         weight_grad(hidden, grad_low),
         rewards,
     )
+
+
+MESH = pl.DeviceIdType.MESH
+STRIP = 16
+
+
+def forward_kernel(
+    tok, low, head, gate_hbm, up_hbm, down_hbm, diff,
+    tok_out, low_out, hidden_out, gate_grad_out, up_grad_out, reward_out, coef_out,
+    weight, tok_all, low_all, head_all, part, sent, got, hidden, gate_grad, up_grad,
+    head_part, head_got, terms, terms_got,
+    weight_sem, z_send, z_recv, head_send, head_recv, y_send, y_recv, core_send, core_recv,
+    x_send, x_recv, v_send, v_recv, r_send, r_recv, out_sem,
+):
+    rows, width = tok.shape
+    units = weight.shape[1]
+    me = lax.axis_index("gx")
+    z = lax.axis_index("gy")
+    x = lax.axis_index("gz")
+    core_peer = me + 1 - 2 * lax.rem(me, 2)
+    y_peer = lax.rem(me + 2, 4)
+    z_from = [z, z + 1 - 2 * lax.rem(z, 2), lax.rem(z + 2, 4), 3 - z]
+    chunk_owner = [me, core_peer, y_peer, 3 - me]
+    x_peer = 1 - x
+
+    def remote(src, dst, send, recv, **peer):
+        return pltpu.make_async_remote_copy(
+            src_ref=src, dst_ref=dst, send_sem=send, recv_sem=recv,
+            device_id=peer, device_id_type=MESH,
+        )
+
+    weight_copies = [
+        pltpu.make_async_copy(ref, weight.at[m], weight_sem.at[m])
+        for m, ref in enumerate((gate_hbm, up_hbm, down_hbm))
+    ]
+    for m in (2, 0, 1):
+        weight_copies[m].start()
+
+    barrier = pltpu.get_barrier_semaphore()
+    peers = [{"gy": z_from[j]} for j in (1, 2, 3)]
+    peers += [{"gx": core_peer}, {"gx": y_peer}, {"gz": x_peer}]
+    for peer in peers:
+        pl.semaphore_signal(barrier, inc=1, device_id=peer, device_id_type=MESH)
+    pl.semaphore_wait(barrier, len(peers))
+
+    own = pl.ds(0, rows)
+    other = pl.ds(rows, rows)
+    pending = []
+
+    def z_copies(a, shard, full):
+        sends = [
+            remote(shard, full.at[0, z, own], z_send.at[a, j - 1], z_recv.at[a, j - 1], gy=z_from[j])
+            for j in (1, 2, 3)
+        ]
+        recvs = [
+            remote(shard, full.at[0, z_from[j], own], z_send.at[a, j - 1], z_recv.at[a, j - 1],
+                   gy=z_from[j])
+            for j in (1, 2, 3)
+        ]
+        return sends, recvs
+
+    def y_copies(a, full):
+        return [
+            remote(full.at[0, z_from[j], own], full.at[1, z_from[j], own],
+                   y_send.at[a, j], y_recv.at[a, j], gx=y_peer)
+            for j in range(4)
+        ]
+
+    def core_copies(a, full):
+        return [
+            remote(full.at[h, :, own], full.at[h, :, other],
+                   core_send.at[a, h], core_recv.at[a, h], gx=core_peer)
+            for h in range(2)
+        ]
+
+    tok_z, tok_z_recv = z_copies(0, tok, tok_all)
+    low_z, low_z_recv = z_copies(1, low, low_all)
+    tok_y, low_y = y_copies(0, tok_all), y_copies(1, low_all)
+    tok_core, low_core = core_copies(0, tok_all), core_copies(1, low_all)
+
+    head_z = [
+        remote(head, head_all.at[z], head_send.at[j - 1], head_recv.at[j - 1], gy=z_from[j])
+        for j in (1, 2, 3)
+    ]
+    head_z_recv = [
+        remote(head, head_all.at[z_from[j]], head_send.at[j - 1], head_recv.at[j - 1], gy=z_from[j])
+        for j in (1, 2, 3)
+    ]
+    for copy in head_z + tok_z:
+        copy.start()
+    tok_all[0, z, 0:rows] = tok[...]
+    tok_y[0].start()
+    low_all[0, z, 0:rows] = low[...]
+    head_all[z] = head[...]
+    part[...] = jnp.zeros_like(part)
+    head_part[...] = jnp.zeros_like(head_part)
+
+    def columns(k):
+        return pl.ds(pl.multiple_of(k * width, width), width)
+
+    def product(full, h, m):
+        @pl.loop(0, 4)
+        def _(k):
+            part[m, h] += lax.dot_general(
+                full[h, k], weight[m, :, columns(k)], (((1,), (1,)), ((), ())),
+                preferred_element_type=jnp.float32,
+            )
+
+        sent[m, h] = part[m, h].astype(jnp.bfloat16)
+        x_copies[m][h].start()
+
+    x_copies = [
+        [
+            remote(sent.at[m, h], got.at[m, h], x_send.at[m, h], x_recv.at[m, h], gz=x_peer)
+            for h in range(2)
+        ]
+        for m in range(3)
+    ]
+
+    for copy in head_z_recv:
+        copy.wait_recv()
+    weight_copies[2].wait()
+
+    @pl.loop(0, 4)
+    def _(k):
+        head_part[...] += lax.dot_general(
+            head_all[k], weight[2, :, columns(k)], (((1,), (1,)), ((), ())),
+            preferred_element_type=jnp.float32,
+        )
+
+    head_copy = remote(head_part, head_got, v_send, v_recv, gz=x_peer)
+    head_copy.start()
+
+    for j in (1, 2, 3):
+        tok_z_recv[j - 1].wait_recv()
+        tok_y[j].start()
+    tok_core[0].start()
+    for copy in low_z:
+        copy.start()
+    weight_copies[0].wait()
+    tok_core[0].wait_recv()
+    product(tok_all, 0, 0)
+    weight_copies[1].wait()
+    product(tok_all, 0, 1)
+
+    for copy in tok_y:
+        copy.wait_recv()
+    tok_core[1].start()
+    low_y[0].start()
+    tok_core[1].wait_recv()
+    tok_stores = [
+        pltpu.make_async_copy(
+            tok_all.at[:, k], tok_out.at[:, :, pl.ds(k * width, width)], out_sem.at[k]
+        )
+        for k in range(4)
+    ]
+    for copy in tok_stores:
+        copy.start()
+    product(tok_all, 1, 0)
+    product(tok_all, 1, 1)
+
+    for j in (1, 2, 3):
+        low_z_recv[j - 1].wait_recv()
+        low_y[j].start()
+    low_core[0].start()
+    low_core[0].wait_recv()
+    product(low_all, 0, 2)
+
+    def activate(h):
+        x_copies[0][h].wait_recv()
+        x_copies[1][h].wait_recv()
+
+        @pl.loop(0, 2 * rows // STRIP)
+        def _(i):
+            strip = pl.ds(pl.multiple_of(i * STRIP, STRIP), STRIP)
+            gate_sum = part[0, h, strip] + got[0, h, strip].astype(jnp.float32)
+            up_sum = part[1, h, strip] + got[1, h, strip].astype(jnp.float32)
+            gate_sigmoid = jax.nn.sigmoid(gate_sum)
+            silu_gate = gate_sum * gate_sigmoid
+            hidden[h, strip] = (silu_gate * up_sum).astype(jnp.bfloat16)
+            part[0, h, strip] = silu_gate
+            part[1, h, strip] = up_sum * gate_sigmoid * (1.0 + gate_sum * (1.0 - gate_sigmoid))
+
+    activate(0)
+    for copy in low_y:
+        copy.wait_recv()
+    low_core[1].start()
+    low_core[1].wait_recv()
+    product(low_all, 1, 2)
+    activate(1)
+    hidden_store = pltpu.make_async_copy(hidden, hidden_out, out_sem.at[4])
+    hidden_store.start()
+
+    lane = lax.broadcasted_iota(jnp.int32, (8, 128), 1)
+    last = pl.ds(rows - STRIP, STRIP)
+    own_term = jnp.sum(
+        tok[last].astype(jnp.float32)[STRIP - 1:] * head[...].astype(jnp.float32)[0:1],
+        axis=1, keepdims=True,
+    )
+    tile = jnp.zeros((8, 128), jnp.float32)
+    for c in range(4):
+        rows_c = pl.ds((c % 2) * rows + rows - STRIP, STRIP)
+        term = jnp.sum(
+            hidden[c // 2, rows_c].astype(jnp.float32)[STRIP - 1:] * head_part[0:1],
+            axis=1, keepdims=True,
+        )
+        if c == 0:
+            term = term + own_term
+        tile = tile + jnp.where(lane == chunk_owner[c], jnp.broadcast_to(term, (8, 128)), 0.0)
+    steps = [{"gz": x_peer}, {"gx": core_peer}, {"gx": y_peer}, {"gy": z_from[1]}, {"gy": z_from[2]}]
+    for k, peer in enumerate(steps):
+        terms[k] = tile
+        copy = remote(terms.at[k], terms_got.at[k], r_send.at[k], r_recv.at[k], **peer)
+        copy.start()
+        copy.wait_recv()
+        pending.append(copy)
+        tile = tile + terms_got[k]
+    reward_out[...] = tile
+    pair_weight = jax.nn.sigmoid(jnp.sum(diff[...] * tile, axis=1, keepdims=True))
+    coefs = reward_weight * jnp.sum(diff[...] * pair_weight, axis=0, keepdims=True)
+    coefs = jnp.broadcast_to(coefs, (8, 128))
+    coef_out[...] = coefs
+    chunk_coef = [
+        jnp.sum(jnp.where(lane == chunk_owner[c], coefs, 0.0), axis=1, keepdims=True)[0:1]
+        for c in range(4)
+    ]
+
+    row = lax.broadcasted_iota(jnp.int32, (STRIP, 1), 0)
+
+    for copy in low_y + low_core:
+        copy.wait_send()
+    for c in range(4):
+        rows_c = pl.ds((c % 2) * rows + rows - STRIP, STRIP)
+        scale = jnp.where(row == STRIP - 1, chunk_coef[c], 0.0)
+        for k in range(4):
+            value = low_all[c // 2, k, rows_c].astype(jnp.float32)
+            value = value + scale * head_all[k].astype(jnp.float32)
+            low_all[c // 2, k, rows_c] = value.astype(jnp.bfloat16)
+    low_stores = [
+        pltpu.make_async_copy(
+            low_all.at[:, k], low_out.at[:, :, pl.ds(k * width, width)], out_sem.at[5 + k]
+        )
+        for k in range(4)
+    ]
+    for copy in low_stores:
+        copy.start()
+
+    head_copy.wait_recv()
+    head_sum = head_part[0:1] + head_got[0:1]
+    for h in range(2):
+        x_copies[2][h].wait_recv()
+        for b in range(2):
+            coef = chunk_coef[2 * h + b]
+
+            @pl.loop(b * rows // STRIP, (b + 1) * rows // STRIP)
+            def _(i):
+                strip = pl.ds(pl.multiple_of(i * STRIP, STRIP), STRIP)
+                at = row + (i * STRIP - b * rows)
+                scale = jnp.where(at == rows - 1, coef, 0.0)
+                grad = part[2, h, strip] + got[2, h, strip].astype(jnp.float32)
+                grad = grad + scale * head_sum
+                up_grad[h, strip] = (grad * part[0, h, strip]).astype(jnp.bfloat16)
+                gate_grad[h, strip] = (grad * part[1, h, strip]).astype(jnp.bfloat16)
+
+    stores = [
+        pltpu.make_async_copy(gate_grad, gate_grad_out, out_sem.at[9]),
+        pltpu.make_async_copy(up_grad, up_grad_out, out_sem.at[10]),
+    ]
+    for copy in stores:
+        copy.start()
+    for copy in head_z + tok_z + low_z + tok_y + tok_core + [head_copy] + pending:
+        copy.wait_send()
+    for copies in x_copies:
+        for copy in copies:
+            copy.wait_send()
+    for copy in tok_stores + low_stores + stores + [hidden_store]:
+        copy.wait()
+
+
+def forward_call(tokens, low, head, gate_weight, up_weight, down_weight, diff):
+    rows, width = tokens.shape
+    units, features = gate_weight.shape
+    low_type, f32 = jnp.bfloat16, jnp.float32
+    struct = jax.ShapeDtypeStruct
+    vmem = pl.BlockSpec(memory_space=pltpu.VMEM)
+    hbm = pl.BlockSpec(memory_space=pl.ANY)
+    dma = pltpu.SemaphoreType.DMA
+    flops = 6 * 4 * rows * units * features
+    return pl.pallas_call(
+        forward_kernel,
+        out_shape=[
+            struct((2, 2 * rows, features), low_type),
+            struct((2, 2 * rows, features), low_type),
+            struct((2, 2 * rows, units), low_type),
+            struct((2, 2 * rows, units), low_type),
+            struct((2, 2 * rows, units), low_type),
+            struct((8, 128), f32),
+            struct((8, 128), f32),
+        ],
+        in_specs=[vmem, vmem, vmem, hbm, hbm, hbm, vmem],
+        out_specs=[hbm, hbm, hbm, hbm, hbm, vmem, vmem],
+        scratch_shapes=[
+            pltpu.VMEM((3, units, features), low_type),
+            pltpu.VMEM((2, 4, 2 * rows, width), low_type),
+            pltpu.VMEM((2, 4, 2 * rows, width), low_type),
+            pltpu.VMEM((4, 16, width), low_type),
+            pltpu.VMEM((3, 2, 2 * rows, units), f32),
+            pltpu.VMEM((3, 2, 2 * rows, units), low_type),
+            pltpu.VMEM((3, 2, 2 * rows, units), low_type),
+            pltpu.VMEM((2, 2 * rows, units), low_type),
+            pltpu.VMEM((2, 2 * rows, units), low_type),
+            pltpu.VMEM((2, 2 * rows, units), low_type),
+            pltpu.VMEM((16, units), f32),
+            pltpu.VMEM((16, units), f32),
+            pltpu.VMEM((5, 8, 128), f32),
+            pltpu.VMEM((5, 8, 128), f32),
+            dma((3,)), dma((2, 3)), dma((2, 3)), dma((3,)), dma((3,)),
+            dma((2, 4)), dma((2, 4)), dma((2, 2)), dma((2, 2)),
+            dma((3, 2)), dma((3, 2)), dma(()), dma(()), dma((5,)), dma((5,)), dma((11,)),
+        ],
+        compiler_params=pltpu.CompilerParams(
+            collective_id=0, has_side_effects=True, vmem_limit_bytes=58 * 1024 * 1024
+        ),
+        cost_estimate=pl.CostEstimate(
+            flops=flops, bytes_accessed=3 * units * features * 2, transcendentals=0
+        ),
+    )(tokens, low, head, gate_weight, up_weight, down_weight, diff)
+
+
+def kernel_body(tokens, gate_weight, up_weight, down_weight, reward_head, lm_grad, pair_index):
+    rows, width = tokens.shape
+    units, features = gate_weight.shape
+    me = lax.axis_index("gx")
+    seq_total = lax.axis_size("gx")
+    sequence = jnp.arange(128, dtype=jnp.int32)
+    diff = (pair_index[:, 1:2] == sequence[None, :]).astype(jnp.float32) - (
+        pair_index[:, 0:1] == sequence[None, :]
+    ).astype(jnp.float32)
+    diff = jnp.pad(diff, ((0, 8 - diff.shape[0]), (0, 0)))
+    head = jnp.broadcast_to(reward_head[None, :], (16, width))
+    tok_all, low_all, hidden, gate_grad, up_grad, reward_tile, coef_tile = forward_call(
+        tokens, lm_grad.astype(jnp.bfloat16), head, gate_weight, up_weight, down_weight, diff
+    )
+    tok_all = tok_all.reshape(4 * rows, features)
+    low_all = low_all.reshape(4 * rows, features)
+    hidden = hidden.reshape(4 * rows, units)
+    gate_grad = gate_grad.reshape(4 * rows, units)
+    up_grad = up_grad.reshape(4 * rows, units)
+    own_coef = lax.dynamic_index_in_dim(coef_tile[0], me, 0, keepdims=False)
+
+    def token_product(chunk):
+        gate_rows = lax.slice_in_dim(gate_grad.reshape(2, 2, rows, units), chunk, chunk + 1, axis=1)
+        up_rows = lax.slice_in_dim(up_grad.reshape(2, 2, rows, units), chunk, chunk + 1, axis=1)
+        return jnp.dot(
+            gate_rows.reshape(2 * rows, units), gate_weight, preferred_element_type=jnp.float32
+        ) + jnp.dot(up_rows.reshape(2 * rows, units), up_weight, preferred_element_type=jnp.float32)
+
+    far = swap(token_product(1).astype(jnp.bfloat16), "gx", 1)
+    near = token_product(0) + far.astype(jnp.float32)
+    y_got = swap(near[rows:].astype(jnp.bfloat16), "gx", 2)
+    blocks = (near[:rows] + y_got.astype(jnp.float32)).reshape(rows, 4, width)
+    gy_me = lax.axis_index("gy")
+    token_sum = lax.dynamic_index_in_dim(blocks, gy_me, 1, keepdims=False)
+    for j in range(1, 4):
+        block = lax.dynamic_index_in_dim(blocks, gy_me ^ j, 1, keepdims=False)
+        token_sum = token_sum + swap(block.astype(jnp.bfloat16), "gy", j).astype(jnp.float32)
+    is_last = (jnp.arange(rows) == rows - 1).astype(jnp.float32)
+    head_term = own_coef * reward_head.astype(jnp.float32)
+    grad_tokens = lm_grad + is_last[:, None] * head_term[None, :] + token_sum
+    loss_scale = 1.0 / jnp.sqrt(jnp.float32(4 * rows))
+
+    def weight_grad(left, right):
+        return jnp.einsum("tf,td->fd", left, right, preferred_element_type=jnp.float32) * loss_scale
+
+    return (
+        grad_tokens,
+        weight_grad(gate_grad, tok_all),
+        weight_grad(up_grad, tok_all),
+        weight_grad(hidden, low_all),
+        reward_tile[0, :seq_total],
+    )
+
+
+def body(*args):
+    sizes = tuple(lax.axis_size(axis) for axis in ("gx", "gy", "gz"))
+    if sizes == (4, 4, 2) and args[0].shape[0] == SEQ_LEN:
+        return kernel_body(*args)
+    return permute_body(*args)
 
 
 def solution(mesh):

time: 266 us -> 213 us (0.80); the launches traced: 262 us -> 213 us
  Pallas kernels: 0 us -> 109 us
  starting transfers between devices: 53.7 us -> 6.23 us
  waiting for transfers between devices: 80.2 us -> 36.8 us
  matrix products: 81.5 us -> 40.3 us
  other arithmetic: 36.5 us -> 6.29 us
  local copies, waits for them, and re-layouts: 8.17 us -> 13.2 us
    pallas_call x0 -> x1, Pallas kernels: none -> 109 us  [forward_call(): pl.pallas_call(forward_kernel, out_shape=[struct((2, 2 * rows, features),...]
    ppermute x36 -> x5, starting transfers between devices: 53.7 us -> 6.23 us  [swap(): return lax.ppermute(value, axis, [(i, i ^ bit) for i in range(size)])]
    ppermute x36 -> x5, waiting for transfers between devices: 80.2 us -> 36.8 us  [swap(): return lax.ppermute(value, axis, [(i, i ^ bit) for i in range(size)])]
    dot_general x9 -> x4, matrix products: 47.2 us -> 17.5 us  [the longest x2 11.2 us: token_product(): jnp.dot(gate_rows.reshape(2 * rows, units), gate_weight, preferred_elemen...]
    concatenate x4 -> x0, other arithmetic: 26.2 us -> none  [the longest x2 26 us: gather_halves(): first = jnp.concatenate([ordered_features(row) for row in pieces], axis=0)]
    dot_general x3, matrix products: 34.3 us -> 22.8 us  [weight_grad(): jnp.einsum('tf,td->fd', left, right, preferred_element_type=jnp.float32)]
    slice x4 -> x5, local copies, waits for them, and re-layouts: 0.59 us -> 4.39 us  [the longest x1 1.39 us: token_product(): lax.slice_in_dim(gate_grad.reshape(2, 2, rows, units), chunk, chunk + 1,...]
  transfers between devices with their start and end apart: 36 -> 5, of which waited for: 16 -> 3; matrix products, arithmetic and copies ran while one was open for 37% -> 15% of each run, Pallas kernels for 0% -> 0%
where the time goes in v2:
time: 213 us
  Pallas kernels  109 us (51%)
  matrix products  40.3 us (19%)
  waiting for transfers between devices  36.8 us (17%)
  local copies, waits for them, and re-layouts  13.2 us (6%)
  other arithmetic  6.29 us (3%)
  starting transfers between devices  6.23 us (3%)
    pallas_call x1, Pallas kernels, forward_call(): pl.pallas_call(forward_kernel, out_shape=[struct((2, 2 * rows, features),...  109 us
    ppermute x5, waiting for transfers between devices, swap(): return lax.ppermute(value, axis, [(i, i ^ bit) for i in range(size)])  36.8 us
    dot_general x3, matrix products, weight_grad(): jnp.einsum('tf,td->fd', left, right, preferred_element_type=jnp.float32)  22.8 us
    dot_general x2, matrix products, token_product(): jnp.dot(gate_rows.reshape(2 * rows, units), gate_weight, preferred_elemen...  11.2 us
    dot_general x2, matrix products, token_product(): jnp.dot(up_rows.reshape(2 * rows, units), up_weight, preferred_element_ty...  6.24 us
    ppermute x5, starting transfers between devices, swap(): return lax.ppermute(value, axis, [(i, i ^ bit) for i in range(size)])  6.23 us
  transfers between devices with their start and end apart: 5, of which 3 were waited for; matrix products, arithmetic and copies ran while one was open for 15% of the time, Pallas kernels for 0%

profile of v2, /device:TPU:0, one launch (start us, length us, event | category | flops | bytes accessed | tf_op | source)
XLA Modules:
  0.0 213.1 jit_solution(4781793524888760701)
XLA Ops:
  0.6 1.0 slice_reduce_fusion.1
  1.6 1.8 convert_element_type.59.low
  4.1 1.3 broadcast_in_dim.2.head
  5.4 109.4 %shard_map.110 = (bf16[2,256,4096]{2,1,0:T(8,128)(2,1)}, bf16[2,256,4096]{2,1,0:T(8,128)(2,1)}, bf16[2,256,896]{2,1,0:T(8,128)(2,1)}, bf16[2,256,896]{2,1,0:T(8,...) custom-call(bf16[128,1024]{1,0:T(8,128)(2,1)} %tok.1, ...), custom_call_target="tpu_custom_call" | custom-call | flops 11274289152 | bytes 22020096 | tf_op jit(solution)/shard_map/pallas_call | solution.py:460
  114.8 1.2 fusion.8
  116.0 1.4 fusion.9
  117.4 5.6 %fusion.11 = f32[256,4096]{1,0:T(8,128)S(1)} fusion(bf16[256,896]{1,0:T(8,128)(2,1)S(1)} %bitcast.54, bf16[896,4096]{1,0:T(8,128)(2,1)} %gate_hbm.1), kind=kOutput, calls=%fused_computation.35 | convolution fusion | flops 1879048192 | bytes 11993088 | tf_op jit(solution)/shard_map/dot_general | solution.py:525
  123.1 3.7 %fusion = bf16[256,4096]{1,0:T(8,128)(2,1)} fusion(f32[256,4096]{1,0:T(8,128)S(1)} %fusion.11, bf16[256,896]{1,0:T(8,128)(2,1)S(1)} %bitcast.55, bf16[896,4096]{1,0:T(8,128)(2,1)S(1)} %bitcast.47), kind=kOutput, calls=%fused_computation.5 | convolution fusion | flops 1881145344 | bytes 14090240 | tf_op jit(solution)/shard_map/dot_general | solution.py:527
  126.8 7.6 %bitcast_multiply_fusion.2 = f32[896,4096]{1,0:T(8,128)} fusion(bf16[2,256,896]{2,1,0:T(8,128)(2,1)S(1)} %copy-done.4, bf16[2,256,4096]{2,1,0:T(8,128)(2,1)S(1)} %copy-done), kind=kOutput, calls=%fused_computation.2 | convolution fusion | flops 3761766400 | bytes 19791872 | tf_op jit(solution)/shard_map/tf,td->fd/dot_general | solution.py:544
  136.4 5.6 %fusion.10 = f32[256,4096]{1,0:T(8,128)S(1)} fusion(bf16[256,896]{1,0:T(8,128)(2,1)S(1)} %bitcast.53, bf16[896,4096]{1,0:T(8,128)(2,1)} %gate_hbm.1), kind=kOutput, calls=%fused_computation.34 | convolution fusion | flops 1879048192 | bytes 11993088 | tf_op jit(solution)/shard_map/dot_general | solution.py:525
  142.0 7.6 %bitcast_multiply_fusion.1 = f32[896,4096]{1,0:T(8,128)} fusion(bf16[2,256,896]{2,1,0:T(8,128)(2,1)S(1)} %copy-done.3, bf16[2,256,4096]{2,1,0:T(8,128)(2,1)S(1)} %copy-done.1), kind=kOutput, calls=%fused_computation.1 | convolution fusion | flops 3761766400 | bytes 19791872 | tf_op jit(solution)/shard_map/tf,td->fd/dot_general | solution.py:544
  149.6 2.6 %convert_add_fusion = f32[256,4096]{1,0:T(8,128)S(1)} fusion(bf16[256,4096]{1,0:T(8,128)(2,1)S(1)} %collective-permute-done, f32[256,4096]{1,0:T(8,128)S(1)} %fusion.10, bf16[256,896]{1,0:T(8,128)(2,1)S(1)} %bitcast.52, bf16[896,4096]{1,0:T(8,128)(2,1)S(1)} %bitcast.49), kind=kOutput, calls=%fused_computation.6 | convolution fusion | flops 1882193920 | bytes 18284544 | tf_op jit(solution)/shard_map/dot_general | solution.py:527
  152.3 1.1 collective-permute-start.1
  153.4 7.6 %bitcast_multiply_fusion = f32[896,4096]{1,0:T(8,128)} fusion(bf16[2,256,896]{2,1,0:T(8,128)(2,1)S(1)} %copy-done.6, bf16[2,256,4096]{2,1,0:T(8,128)(2,1)S(1)} %copy-done.2), kind=kOutput, calls=%fused_computation | convolution fusion | flops 3761766400 | bytes 19791872 | tf_op jit(solution)/shard_map/tf,td->fd/dot_general | solution.py:544
  161.0 16.9 %collective-permute-done.1 = bf16[128,4096]{1,0:T(8,128)(2,1)S(1)} collective-permute-done((bf16[128,4096]{1,0:T(8,128)(2,1)S(1)}, bf16[128,4096]{1,0:T(8,128)(2,1)S(1)}, u32[]{:S(2)}, u32[]{:S(2)}) %collective-permute-start.1) | collective-permute-done | bytes 1048608 | tf_op jit(solution)/shard_map/ppermute | solution.py:16
  178.0 1.6 slice_add_fusion
  179.6 2.7 %reshape.46 = f32[128,4,1024]{2,1,0:T(4,128)S(1)} reshape(f32[128,4096]{1,0:T(8,128)} %slice_add_fusion) | data formatting | bytes 4194304 | tf_op jit(solution)/shard_map/reshape | solution.py:532
  182.3 1.6 constant_dynamic-slice_fusion.2
  184.2 2.1 collective-permute-start.4
  186.3 3.0 %collective-permute-start.3 = (bf16[128,1024]{1,0:T(8,128)(2,1)S(1)}, bf16[128,1024]{1,0:T(8,128)(2,1)}, u32[]{:S(2)}, u32[]{:S(2)}) collective-permute-start(bf16[128,1024]{1,0:T(8,128)(2,1)S(1)} %bitcast.57), channel_id=1, source_target_pairs={{0,4},{2,6},{4,0},{6,2},{1,5},{3,7},{5,1},{7,3},{8,12},{10,14},{12... | collective-permute-start | bytes 786440 | tf_op jit(solution)/shard_map/ppermute | solution.py:16
  189.3 1.2 slice_bitcast_fusion
  191.0 4.4 %collective-permute-done.4 = bf16[128,1024]{1,0:T(8,128)(2,1)} collective-permute-done((bf16[128,1024]{1,0:T(8,128)(2,1)S(1)}, bf16[128,1024]{1,0:T(8,128)(2,1)}, u32[]{:S(2)}, u32[]{:S(2)}) %collective-permute-start.4) | collective-permute-done | bytes 262176 | tf_op jit(solution)/shard_map/ppermute | solution.py:16
  195.5 15.4 %collective-permute-done.3 = bf16[128,1024]{1,0:T(8,128)(2,1)} collective-permute-done((bf16[128,1024]{1,0:T(8,128)(2,1)S(1)}, bf16[128,1024]{1,0:T(8,128)(2,1)}, u32[]{:S(2)}, u32[]{:S(2)}) %collective-permute-start.3) | collective-permute-done | bytes 262176 | tf_op jit(solution)/shard_map/ppermute | solution.py:16
  210.9 2.2 %fusion.3 = f32[128,1024]{1,0:T(8,128)} fusion(f32[128,1,1024]{2,1,0:T(1,128)S(1)} %constant_dynamic-slice_fusion.3, bf16[128,1024]{1,0:T(8,128)(2,1)} %collective-permute-done.4, bf16[128,1024]{1,0:T(8,128)(2,1)} %collective-permute-done.3, bf16[128,1024]{1,0:T(8,128)(2,1)} %collective-permute-done.2, f32[128,1024]{1,0:T(8,128)S(1)} %copy-done.5, ...), kind=kLoop, calls=%fused_computation.15 | loop fusion | flops 1179648 | bytes 2363904 | tf_op jit(solution)/shard_map/add | solution.py:540
  (41 shorter events, 3.6 us)
Async XLA Ops:
  116.0 7.1 %slice-start = ((s8[7340032]{0:T(1024)(128)(4,1)}), s8[4194304]{0:T(1024)(128)(4,1)S(1)}, s32[]{:S(2)}) async-start(s8[7340032]{0:T(1024)(128)(4,1)} %bitcast.46), calls=%async_computation | async-start | bytes 8388608
  117.4 5.7 %slice-start.1 = ((s8[7340032]{0:T(1024)(128)(4,1)}), s8[3145728]{0:T(1024)(128)(4,1)S(1)}, s32[]{:S(2)}) async-start(s8[7340032]{0:T(1024)(128)(4,1)} %bitcast.46), calls=%async_computation.1 | async-start | bytes 6291456
  123.1 3.7 %copy-start = (bf16[2,256,4096]{2,1,0:T(8,128)(2,1)S(1)}, bf16[2,256,4096]{2,1,0:T(8,128)(2,1)}, u32[]{:S(2)}) copy-start(bf16[2,256,4096]{2,1,0:T(8,128)(2,1)} %get-tuple-element.15) | copy-start | bytes 12582916
  123.1 3.7 %copy-start.4 = (bf16[2,256,896]{2,1,0:T(8,128)(2,1)S(1)}, bf16[2,256,896]{2,1,0:T(8,128)(2,1)}, u32[]{:S(2)}) copy-start(bf16[2,256,896]{2,1,0:T(8,128)(2,1)} %get-tuple-element.13) | copy-start | bytes 2752516
  126.8 22.8 %collective-permute-start = (bf16[256,4096]{1,0:T(8,128)(2,1)}, bf16[256,4096]{1,0:T(8,128)(2,1)S(1)}, u32[]{:S(2)}, u32[]{:S(2)}) collective-permute-start(bf16[256,4096]{1,0:T(8,128)(2,1)} %fusion), channel_id=1, source_target_pairs={{0,8},{8,0},{16,24},{24,16},{1,9},{9,1},{17,25},{25,17},{2,10},{10... | collective-permute-start | bytes 6291464 | tf_op jit(solution)/shard_map/ppermute | solution.py:16
  126.8 8.9 %copy-start.7 = (bf16[1024]{0:T(1024)(128)(2,1)S(1)}, bf16[1024]{0:T(1024)(128)(2,1)}, u32[]{:S(2)}) copy-start(bf16[1024]{0:T(1024)(128)(2,1)} %param.11) | copy-start | bytes 6148
  136.3 5.6 %copy-start.1 = (bf16[2,256,4096]{2,1,0:T(8,128)(2,1)S(1)}, bf16[2,256,4096]{2,1,0:T(8,128)(2,1)}, u32[]{:S(2)}) copy-start(bf16[2,256,4096]{2,1,0:T(8,128)(2,1)} %get-tuple-element.15) | copy-start | bytes 12582916
  136.4 5.6 %copy-start.3 = (bf16[2,256,896]{2,1,0:T(8,128)(2,1)S(1)}, bf16[2,256,896]{2,1,0:T(8,128)(2,1)}, u32[]{:S(2)}) copy-start(bf16[2,256,896]{2,1,0:T(8,128)(2,1)} %get-tuple-element.14) | copy-start | bytes 2752516
  136.4 13.2 %slice-start.2 = ((s8[7340032]{0:T(1024)(128)(4,1)}), s8[4194304]{0:T(1024)(128)(4,1)S(1)}, s32[]{:S(2)}) async-start(s8[7340032]{0:T(1024)(128)(4,1)} %bitcast.48), calls=%async_computation.2 | async-start | bytes 8388608
  142.0 7.6 %slice-start.3 = ((s8[7340032]{0:T(1024)(128)(4,1)}), s8[3145728]{0:T(1024)(128)(4,1)S(1)}, s32[]{:S(2)}) async-start(s8[7340032]{0:T(1024)(128)(4,1)} %bitcast.48), calls=%async_computation.3 | async-start | bytes 6291456
  149.6 3.8 %copy-start.2 = (bf16[2,256,4096]{2,1,0:T(8,128)(2,1)S(1)}, bf16[2,256,4096]{2,1,0:T(8,128)(2,1)}, u32[]{:S(2)}) copy-start(bf16[2,256,4096]{2,1,0:T(8,128)(2,1)} %get-tuple-element.17) | copy-start | bytes 12582916
  149.6 3.8 %copy-start.6 = (bf16[2,256,896]{2,1,0:T(8,128)(2,1)S(1)}, bf16[2,256,896]{2,1,0:T(8,128)(2,1)}, u32[]{:S(2)}) copy-start(bf16[2,256,896]{2,1,0:T(8,128)(2,1)} %get-tuple-element.16) | copy-start | bytes 2752516
  152.3 25.6 %collective-permute-start.1 = (bf16[128,4096]{1,0:T(8,128)(2,1)S(1)}, bf16[128,4096]{1,0:T(8,128)(2,1)S(1)}, u32[]{:S(2)}, u32[]{:S(2)}) collective-permute-start(bf16[128,4096]{1,0:T(8,128)(2,1)S(1)} %slice.52), channel_id=1, source_target_pairs={{0,16},{8,24},{16,0},{24,8},{1,17},{9,25},{17,1},{25,9},{2,18},{10... | collective-permute-start | bytes 3145736 | tf_op jit(solution)/shard_map/ppermute | solution.py:16
  182.2 28.7 %copy-start.5 = (f32[128,1024]{1,0:T(8,128)S(1)}, f32[128,1024]{1,0:T(8,128)}, u32[]{:S(2)}) copy-start(f32[128,1024]{1,0:T(8,128)} %param.12) | copy-start | bytes 1572868
  184.2 11.3 %collective-permute-start.4 = (bf16[128,1024]{1,0:T(8,128)(2,1)S(1)}, bf16[128,1024]{1,0:T(8,128)(2,1)}, u32[]{:S(2)}, u32[]{:S(2)}) collective-permute-start(bf16[128,1024]{1,0:T(8,128)(2,1)S(1)} %bitcast.58), channel_id=1, source_target_pairs={{0,6},{2,4},{4,2},{6,0},{1,7},{3,5},{5,3},{7,1},{8,14},{10,12},{12... | collective-permute-start | bytes 786440 | tf_op jit(solution)/shard_map/ppermute | solution.py:16
  186.3 24.6 %collective-permute-start.3 = (bf16[128,1024]{1,0:T(8,128)(2,1)S(1)}, bf16[128,1024]{1,0:T(8,128)(2,1)}, u32[]{:S(2)}, u32[]{:S(2)}) collective-permute-start(bf16[128,1024]{1,0:T(8,128)(2,1)S(1)} %bitcast.57), channel_id=1, source_target_pairs={{0,4},{2,6},{4,0},{6,2},{1,5},{3,7},{5,1},{7,3},{8,12},{10,14},{12... | collective-permute-start | bytes 786440 | tf_op jit(solution)/shard_map/ppermute | solution.py:16
  189.3 21.6 %collective-permute-start.2 = (bf16[128,1024]{1,0:T(8,128)(2,1)S(1)}, bf16[128,1024]{1,0:T(8,128)(2,1)}, u32[]{:S(2)}, u32[]{:S(2)}) collective-permute-start(bf16[128,1024]{1,0:T(8,128)(2,1)S(1)} %bitcast.56), channel_id=1, source_target_pairs={{0,2},{2,0},{4,6},{6,4},{1,3},{3,1},{5,7},{7,5},{8,10},{10,8},{12,... | collective-permute-start | bytes 786440 | tf_op jit(solution)/shard_map/ppermute | solution.py:16

commit v3 on v2

--- a/solution.py
+++ b/solution.py
@@ -176,12 +176,14 @@
 
 
 def forward_kernel(
-    tok, low, head, gate_hbm, up_hbm, down_hbm, diff,
-    tok_out, low_out, hidden_out, gate_grad_out, up_grad_out, reward_out, coef_out,
+    tok, lm_grad, head_row, gate_hbm, up_hbm, down_hbm, diff,
+    tok_out, low_out, hidden_out, gate_grad_out, up_grad_out, grad_out, reward_out,
+    low, head, keep, core_sent, core_got, y_sent, y_got, z_sent, z_got,
     weight, tok_all, low_all, head_all, part, sent, got, hidden, gate_grad, up_grad,
     head_part, head_got, terms, terms_got,
     weight_sem, z_send, z_recv, head_send, head_recv, y_send, y_recv, core_send, core_recv,
     x_send, x_recv, v_send, v_recv, r_send, r_recv, out_sem,
+    cs_send, cs_recv, ys_send, ys_recv, zs_send, zs_recv,
 ):
     rows, width = tok.shape
     units = weight.shape[1]
@@ -207,6 +209,7 @@
     for m in (2, 0, 1):
         weight_copies[m].start()
 
+    head[...] = jnp.broadcast_to(head_row[...].astype(jnp.float32), head.shape).astype(jnp.bfloat16)
     barrier = pltpu.get_barrier_semaphore()
     peers = [{"gy": z_from[j]} for j in (1, 2, 3)]
     peers += [{"gx": core_peer}, {"gx": y_peer}, {"gz": x_peer}]
@@ -261,6 +264,7 @@
         copy.start()
     tok_all[0, z, 0:rows] = tok[...]
     tok_y[0].start()
+    low[...] = lm_grad[...].astype(jnp.bfloat16)
     low_all[0, z, 0:rows] = low[...]
     head_all[z] = head[...]
     part[...] = jnp.zeros_like(part)
@@ -328,12 +332,11 @@
     for copy in tok_stores:
         copy.start()
     product(tok_all, 1, 0)
-    product(tok_all, 1, 1)
-
     for j in (1, 2, 3):
         low_z_recv[j - 1].wait_recv()
         low_y[j].start()
     low_core[0].start()
+    product(tok_all, 1, 1)
     low_core[0].wait_recv()
     product(low_all, 0, 2)
 
@@ -390,7 +393,6 @@
     pair_weight = jax.nn.sigmoid(jnp.sum(diff[...] * tile, axis=1, keepdims=True))
     coefs = reward_weight * jnp.sum(diff[...] * pair_weight, axis=0, keepdims=True)
     coefs = jnp.broadcast_to(coefs, (8, 128))
-    coef_out[...] = coefs
     chunk_coef = [
         jnp.sum(jnp.where(lane == chunk_owner[c], coefs, 0.0), axis=1, keepdims=True)[0:1]
         for c in range(4)
@@ -418,6 +420,25 @@
 
     head_copy.wait_recv()
     head_sum = head_part[0:1] + head_got[0:1]
+
+    def core_sum(h, j):
+        return remote(core_sent.at[h, z_from[j]], core_got.at[h, z_from[j]],
+                      cs_send.at[h, j], cs_recv.at[h, j], gx=core_peer)
+
+    def y_sum(j):
+        return remote(y_sent.at[z_from[j]], y_got.at[z_from[j]], ys_send.at[j], ys_recv.at[j], gx=y_peer)
+
+    def z_sum(j):
+        return remote(z_sent.at[j - 1], z_got.at[j - 1], zs_send.at[j - 1], zs_recv.at[j - 1],
+                      gy=z_from[j])
+
+    def send_y(j):
+        core_sum(1, j).wait_recv()
+        k = z_from[j]
+        y_sent[k] = (keep[1, k] + core_got[1, k].astype(jnp.float32)).astype(jnp.bfloat16)
+        y_sum(j).start()
+
+    order = (3, 2, 1, 0)
     for h in range(2):
         x_copies[2][h].wait_recv()
         for b in range(2):
@@ -433,12 +454,47 @@
                 up_grad[h, strip] = (grad * part[0, h, strip]).astype(jnp.bfloat16)
                 gate_grad[h, strip] = (grad * part[1, h, strip]).astype(jnp.bfloat16)
 
+        for n, j in enumerate(order):
+            k = z_from[j]
+            value = jnp.dot(
+                gate_grad[h], weight[0, :, columns(k)], preferred_element_type=jnp.float32
+            ) + jnp.dot(up_grad[h], weight[1, :, columns(k)], preferred_element_type=jnp.float32)
+            core_sent[h, k] = value[rows:].astype(jnp.bfloat16)
+            core_sum(h, j).start()
+            keep[h, k] = value[:rows]
+            if h == 1 and n > 0:
+                send_y(order[n - 1])
+    send_y(order[-1])
+
     stores = [
         pltpu.make_async_copy(gate_grad, gate_grad_out, out_sem.at[9]),
         pltpu.make_async_copy(up_grad, up_grad_out, out_sem.at[10]),
     ]
     for copy in stores:
         copy.start()
+    for j in order:
+        k = z_from[j]
+        core_sum(0, j).wait_recv()
+        near = keep[0, k] + core_got[0, k].astype(jnp.float32)
+        y_sum(j).wait_recv()
+        near = near + y_got[k].astype(jnp.float32)
+        if j > 0:
+            z_sent[j - 1] = near.astype(jnp.bfloat16)
+            z_sum(j).start()
+        else:
+            grad_out[...] = lm_grad[...] + near
+    for j in (3, 2, 1):
+        z_sum(j).wait_recv()
+        grad_out[...] += z_got[j - 1].astype(jnp.float32)
+    scale = jnp.where(row == STRIP - 1, chunk_coef[0], 0.0)
+    grad_out[last] += scale * head[...].astype(jnp.float32)
+
+    for j in order:
+        core_sum(0, j).wait_send()
+        core_sum(1, j).wait_send()
+        y_sum(j).wait_send()
+        if j > 0:
+            z_sum(j).wait_send()
     for copy in head_z + tok_z + low_z + tok_y + tok_core + [head_copy] + pending:
         copy.wait_send()
     for copies in x_copies:
@@ -448,7 +504,7 @@
         copy.wait()
 
 
-def forward_call(tokens, low, head, gate_weight, up_weight, down_weight, diff):
+def forward_call(tokens, lm_grad, head_row, gate_weight, up_weight, down_weight, diff):
     rows, width = tokens.shape
     units, features = gate_weight.shape
     low_type, f32 = jnp.bfloat16, jnp.float32
@@ -465,12 +521,21 @@
             struct((2, 2 * rows, units), low_type),
             struct((2, 2 * rows, units), low_type),
             struct((2, 2 * rows, units), low_type),
-            struct((8, 128), f32),
+            struct((rows, width), f32),
             struct((8, 128), f32),
         ],
         in_specs=[vmem, vmem, vmem, hbm, hbm, hbm, vmem],
         out_specs=[hbm, hbm, hbm, hbm, hbm, vmem, vmem],
         scratch_shapes=[
+            pltpu.VMEM((rows, width), low_type),
+            pltpu.VMEM((16, width), low_type),
+            pltpu.VMEM((2, 4, rows, width), f32),
+            pltpu.VMEM((2, 4, rows, width), low_type),
+            pltpu.VMEM((2, 4, rows, width), low_type),
+            pltpu.VMEM((4, rows, width), low_type),
+            pltpu.VMEM((4, rows, width), low_type),
+            pltpu.VMEM((3, rows, width), low_type),
+            pltpu.VMEM((3, rows, width), low_type),
             pltpu.VMEM((3, units, features), low_type),
             pltpu.VMEM((2, 4, 2 * rows, width), low_type),
             pltpu.VMEM((2, 4, 2 * rows, width), low_type),
@@ -488,56 +553,34 @@
             dma((3,)), dma((2, 3)), dma((2, 3)), dma((3,)), dma((3,)),
             dma((2, 4)), dma((2, 4)), dma((2, 2)), dma((2, 2)),
             dma((3, 2)), dma((3, 2)), dma(()), dma(()), dma((5,)), dma((5,)), dma((11,)),
+            dma((2, 4)), dma((2, 4)), dma((4,)), dma((4,)), dma((3,)), dma((3,)),
         ],
         compiler_params=pltpu.CompilerParams(
-            collective_id=0, has_side_effects=True, vmem_limit_bytes=58 * 1024 * 1024
+            collective_id=0, has_side_effects=True, vmem_limit_bytes=62 * 1024 * 1024
         ),
         cost_estimate=pl.CostEstimate(
             flops=flops, bytes_accessed=3 * units * features * 2, transcendentals=0
         ),
-    )(tokens, low, head, gate_weight, up_weight, down_weight, diff)
+    )(tokens, lm_grad, head_row, gate_weight, up_weight, down_weight, diff)
 
 
 def kernel_body(tokens, gate_weight, up_weight, down_weight, reward_head, lm_grad, pair_index):
     rows, width = tokens.shape
     units, features = gate_weight.shape
-    me = lax.axis_index("gx")
     seq_total = lax.axis_size("gx")
     sequence = jnp.arange(128, dtype=jnp.int32)
     diff = (pair_index[:, 1:2] == sequence[None, :]).astype(jnp.float32) - (
         pair_index[:, 0:1] == sequence[None, :]
     ).astype(jnp.float32)
     diff = jnp.pad(diff, ((0, 8 - diff.shape[0]), (0, 0)))
-    head = jnp.broadcast_to(reward_head[None, :], (16, width))
-    tok_all, low_all, hidden, gate_grad, up_grad, reward_tile, coef_tile = forward_call(
-        tokens, lm_grad.astype(jnp.bfloat16), head, gate_weight, up_weight, down_weight, diff
+    tok_all, low_all, hidden, gate_grad, up_grad, grad_tokens, reward_tile = forward_call(
+        tokens, lm_grad, reward_head[None, :], gate_weight, up_weight, down_weight, diff
     )
     tok_all = tok_all.reshape(4 * rows, features)
     low_all = low_all.reshape(4 * rows, features)
     hidden = hidden.reshape(4 * rows, units)
     gate_grad = gate_grad.reshape(4 * rows, units)
     up_grad = up_grad.reshape(4 * rows, units)
-    own_coef = lax.dynamic_index_in_dim(coef_tile[0], me, 0, keepdims=False)
-
-    def token_product(chunk):
-        gate_rows = lax.slice_in_dim(gate_grad.reshape(2, 2, rows, units), chunk, chunk + 1, axis=1)
-        up_rows = lax.slice_in_dim(up_grad.reshape(2, 2, rows, units), chunk, chunk + 1, axis=1)
-        return jnp.dot(
-            gate_rows.reshape(2 * rows, units), gate_weight, preferred_element_type=jnp.float32
-        ) + jnp.dot(up_rows.reshape(2 * rows, units), up_weight, preferred_element_type=jnp.float32)
-
-    far = swap(token_product(1).astype(jnp.bfloat16), "gx", 1)
-    near = token_product(0) + far.astype(jnp.float32)
-    y_got = swap(near[rows:].astype(jnp.bfloat16), "gx", 2)
-    blocks = (near[:rows] + y_got.astype(jnp.float32)).reshape(rows, 4, width)
-    gy_me = lax.axis_index("gy")
-    token_sum = lax.dynamic_index_in_dim(blocks, gy_me, 1, keepdims=False)
-    for j in range(1, 4):
-        block = lax.dynamic_index_in_dim(blocks, gy_me ^ j, 1, keepdims=False)
-        token_sum = token_sum + swap(block.astype(jnp.bfloat16), "gy", j).astype(jnp.float32)
-    is_last = (jnp.arange(rows) == rows - 1).astype(jnp.float32)
-    head_term = own_coef * reward_head.astype(jnp.float32)
-    grad_tokens = lm_grad + is_last[:, None] * head_term[None, :] + token_sum
     loss_scale = 1.0 / jnp.sqrt(jnp.float32(4 * rows))
 
     def weight_grad(left, right):

time: 213 us -> 184 us (0.86)
  Pallas kernels: 109 us -> 150 us
  waiting for transfers between devices: 36.8 us -> 0 us
  matrix products: 40.3 us -> 27.3 us
  local copies, waits for them, and re-layouts: 13.2 us -> 4.84 us
  starting transfers between devices: 6.23 us -> 0 us
  other arithmetic: 6.29 us -> 0.07 us
    pallas_call x1, Pallas kernels: 109 us -> 150 us  [forward_call(): pl.pallas_call(forward_kernel, out_shape=[struct((2, 2 * rows, features),...]
    ppermute x5 -> x0, waiting for transfers between devices: 36.8 us -> none  [swap(): return lax.ppermute(value, axis, [(i, i ^ bit) for i in range(size)])]
    dot_general x4 -> x0, matrix products: 17.5 us -> none  [the longest x2 11.2 us: token_product(): jnp.dot(gate_rows.reshape(2 * rows, units), gate_weight, preferred_elemen...]
    ppermute x5 -> x0, starting transfers between devices: 6.23 us -> none  [swap(): return lax.ppermute(value, axis, [(i, i ^ bit) for i in range(size)])]
    dot_general x3, matrix products: 22.8 us -> 27.3 us  [weight_grad(): jnp.einsum('tf,td->fd', left, right, preferred_element_type=jnp.float32)]
    add x2 -> x0, other arithmetic: 3.78 us -> none  [the longest x1 2.18 us: kernel_body(): grad_tokens = lm_grad + is_last[:, None] * head_term[None, :] + token_sum]
    slice x4 -> x0, local copies, waits for them, and re-layouts: 3.42 us -> none  [the longest x1 1.39 us: token_product(): lax.slice_in_dim(gate_grad.reshape(2, 2, rows, units), chunk, chunk + 1,...]
    dynamic_slice x3 -> x0, local copies, waits for them, and re-layouts: 2.76 us -> none  [the longest x1 1.63 us: kernel_body(): block = lax.dynamic_index_in_dim(blocks, gy_me ^ j, 1, keepdims=False)]
  transfers between devices with their start and end apart: 5 -> 0, of which waited for: 3 -> 0; matrix products, arithmetic and copies ran while one was open for 15% -> 0% of each run, Pallas kernels for 0% -> 0%
where the time goes in v3:
time: 184 us; the launch traced here: 183 us
  Pallas kernels  150 us (82%)
  matrix products  27.3 us (15%)
  local copies, waits for them, and re-layouts  4.84 us (3%)
    pallas_call x1, Pallas kernels, forward_call(): pl.pallas_call(forward_kernel, out_shape=[struct((2, 2 * rows, features),...  150 us
    dot_general x3, matrix products, weight_grad(): jnp.einsum('tf,td->fd', left, right, preferred_element_type=jnp.float32)  27.3 us

profile of v3, /device:TPU:0, one launch (start us, length us, event | category | flops | bytes accessed | tf_op | source)
XLA Modules:
  0.0 183.3 jit_solution(14943140935718242392)
XLA Ops:
  0.6 1.0 slice_reduce_fusion.1
  1.6 0.1 fusion
  1.7 0.6 pad.4.diff
  2.3 1.3 broadcast_in_dim.2.head_row
  3.6 150.4 %shard_map.110 = (bf16[2,256,4096]{2,1,0:T(8,128)(2,1)}, bf16[2,256,4096]{2,1,0:T(8,128)(2,1)}, bf16[2,256,896]{2,1,0:T(8,128)(2,1)}, bf16[2,256,896]{2,1,0:T(8,...) custom-call(bf16[128,1024]{1,0:T(8,128)(2,1)} %tok.1, f32[128,1024]{1,0:T(8,128)} %lm_grad.1, ...), custom_call_target="tpu_custom_call" | custom-call | flops 11274289152 | bytes 22020096 | tf_op jit(solution)/shard_map/pallas_call | solution.py:516
  154.0 1.2 slice_bitcast_fusion
  155.2 0.0 copy-start
  155.2 0.0 copy-start.3
  155.2 12.1 %bitcast_multiply_fusion.2 = f32[896,4096]{1,0:T(8,128)} fusion(bf16[2,256,896]{2,1,0:T(8,128)(2,1)} %get-tuple-element.13, bf16[2,256,4096]{2,1,0:T(8,128)(2,1)} %get-tuple-element.14), kind=kOutput, calls=%fused_computation.2 | convolution fusion | flops 3761766400 | bytes 19791872 | tf_op jit(solution)/shard_map/tf,td->fd/dot_general | solution.py:587
  167.3 0.0 copy-done
  167.3 0.0 copy-done.3
  167.3 0.0 copy-start.1
  167.3 0.0 copy-start.2
  167.3 7.6 %bitcast_multiply_fusion.1 = f32[896,4096]{1,0:T(8,128)} fusion(bf16[2,256,896]{2,1,0:T(8,128)(2,1)S(1)} %copy-done.3, bf16[2,256,4096]{2,1,0:T(8,128)(2,1)S(1)} %copy-done), kind=kOutput, calls=%fused_computation.1 | convolution fusion | flops 3761766400 | bytes 19791872 | tf_op jit(solution)/shard_map/tf,td->fd/dot_general | solution.py:587
  174.9 0.0 copy-done.1
  174.9 0.0 copy-done.2
  174.9 0.0 copy-start.4
  174.9 7.6 %bitcast_multiply_fusion = f32[896,4096]{1,0:T(8,128)} fusion(bf16[2,256,896]{2,1,0:T(8,128)(2,1)S(1)} %copy-done.2, bf16[2,256,4096]{2,1,0:T(8,128)(2,1)S(1)} %copy-done.1), kind=kOutput, calls=%fused_computation | convolution fusion | flops 3761766400 | bytes 19791872 | tf_op jit(solution)/shard_map/tf,td->fd/dot_general | solution.py:587
  182.5 0.0 copy-done.4
  182.5 0.8 copy.19
Async XLA Ops:
  155.2 12.1 %copy-start = (bf16[2,256,4096]{2,1,0:T(8,128)(2,1)S(1)}, bf16[2,256,4096]{2,1,0:T(8,128)(2,1)}, u32[]{:S(2)}) copy-start(bf16[2,256,4096]{2,1,0:T(8,128)(2,1)} %get-tuple-element.14) | copy-start | bytes 12582916
  155.2 12.1 %copy-start.3 = (bf16[2,256,896]{2,1,0:T(8,128)(2,1)S(1)}, bf16[2,256,896]{2,1,0:T(8,128)(2,1)}, u32[]{:S(2)}) copy-start(bf16[2,256,896]{2,1,0:T(8,128)(2,1)} %get-tuple-element.15) | copy-start | bytes 2752516
  167.3 7.6 %copy-start.1 = (bf16[2,256,4096]{2,1,0:T(8,128)(2,1)S(1)}, bf16[2,256,4096]{2,1,0:T(8,128)(2,1)}, u32[]{:S(2)}) copy-start(bf16[2,256,4096]{2,1,0:T(8,128)(2,1)} %get-tuple-element.17) | copy-start | bytes 12582916
  167.3 7.6 %copy-start.2 = (bf16[2,256,896]{2,1,0:T(8,128)(2,1)S(1)}, bf16[2,256,896]{2,1,0:T(8,128)(2,1)}, u32[]{:S(2)}) copy-start(bf16[2,256,896]{2,1,0:T(8,128)(2,1)} %get-tuple-element.16) | copy-start | bytes 2752516
  174.9 7.6 %copy-start.4 = (f32[128,1024]{1,0:T(8,128)S(1)}, f32[128,1024]{1,0:T(8,128)}, u32[]{:S(2)}) copy-start(f32[128,1024]{1,0:T(8,128)} %get-tuple-element.26) | copy-start | bytes 1572868

commit v4 on v3

--- a/solution.py
+++ b/solution.py
@@ -274,19 +274,27 @@
         return pl.ds(pl.multiple_of(k * width, width), width)
 
     def product(full, h, m):
-        @pl.loop(0, 4)
-        def _(k):
-            part[m, h] += lax.dot_general(
-                full[h, k], weight[m, :, columns(k)], (((1,), (1,)), ((), ())),
-                preferred_element_type=jnp.float32,
-            )
-
-        sent[m, h] = part[m, h].astype(jnp.bfloat16)
-        x_copies[m][h].start()
-
+        for n, block in enumerate(unit_blocks):
+
+            @pl.loop(0, 4)
+            def _(k):
+                part[m, h, :, block] += lax.dot_general(
+                    full[h, k], weight[m, block, columns(k)], (((1,), (1,)), ((), ())),
+                    preferred_element_type=jnp.float32,
+                )
+
+            sent[m, h, :, block] = part[m, h, :, block].astype(jnp.bfloat16)
+            x_copies[m][h][n].start()
+
+    first_units = -(-units // 512) * 256
+    unit_blocks = [pl.ds(0, first_units), pl.ds(first_units, units - first_units)]
     x_copies = [
         [
-            remote(sent.at[m, h], got.at[m, h], x_send.at[m, h], x_recv.at[m, h], gz=x_peer)
+            [
+                remote(sent.at[m, h, :, block], got.at[m, h, :, block],
+                       x_send.at[m, h, n], x_recv.at[m, h, n], gz=x_peer)
+                for n, block in enumerate(unit_blocks)
+            ]
             for h in range(2)
         ]
         for m in range(3)
@@ -341,8 +349,8 @@
     product(low_all, 0, 2)
 
     def activate(h):
-        x_copies[0][h].wait_recv()
-        x_copies[1][h].wait_recv()
+        for copy in x_copies[0][h] + x_copies[1][h]:
+            copy.wait_recv()
 
         @pl.loop(0, 2 * rows // STRIP)
         def _(i):
@@ -440,7 +448,8 @@
 
     order = (3, 2, 1, 0)
     for h in range(2):
-        x_copies[2][h].wait_recv()
+        for copy in x_copies[2][h]:
+            copy.wait_recv()
         for b in range(2):
             coef = chunk_coef[2 * h + b]
 
@@ -498,7 +507,7 @@
     for copy in head_z + tok_z + low_z + tok_y + tok_core + [head_copy] + pending:
         copy.wait_send()
     for copies in x_copies:
-        for copy in copies:
+        for copy in copies[0] + copies[1]:
             copy.wait_send()
     for copy in tok_stores + low_stores + stores + [hidden_store]:
         copy.wait()
@@ -552,7 +561,7 @@
             pltpu.VMEM((5, 8, 128), f32),
             dma((3,)), dma((2, 3)), dma((2, 3)), dma((3,)), dma((3,)),
             dma((2, 4)), dma((2, 4)), dma((2, 2)), dma((2, 2)),
-            dma((3, 2)), dma((3, 2)), dma(()), dma(()), dma((5,)), dma((5,)), dma((11,)),
+            dma((3, 2, 2)), dma((3, 2, 2)), dma(()), dma(()), dma((5,)), dma((5,)), dma((11,)),
             dma((2, 4)), dma((2, 4)), dma((4,)), dma((4,)), dma((3,)), dma((3,)),
         ],
         compiler_params=pltpu.CompilerParams(

time: 184 us -> 183 us (level)
  no operation moved by 1% of the time
where the time goes in v4:
time: 183 us; the launch traced here: 182 us
  Pallas kernels  149 us (81%)
  matrix products  27.3 us (15%)
  local copies, waits for them, and re-layouts  4.84 us (3%)
    pallas_call x1, Pallas kernels, forward_call(): pl.pallas_call(forward_kernel, out_shape=[struct((2, 2 * rows, features),...  149 us
    dot_general x3, matrix products, weight_grad(): jnp.einsum('tf,td->fd', left, right, preferred_element_type=jnp.float32)  27.3 us

profile of v4, /device:TPU:0, one launch (start us, length us, event | category | flops | bytes accessed | tf_op | source)
XLA Modules:
  0.0 182.3 jit_solution(4307789158951540619)
XLA Ops:
  0.6 1.0 slice_reduce_fusion.1
  1.6 0.1 fusion
  1.7 0.6 pad.4.diff
  2.3 1.3 broadcast_in_dim.2.head_row
  3.6 149.4 %shard_map.110 = (bf16[2,256,4096]{2,1,0:T(8,128)(2,1)}, bf16[2,256,4096]{2,1,0:T(8,128)(2,1)}, bf16[2,256,896]{2,1,0:T(8,128)(2,1)}, bf16[2,256,896]{2,1,0:T(8,...) custom-call(bf16[128,1024]{1,0:T(8,128)(2,1)} %tok.1, f32[128,1024]{1,0:T(8,128)} %lm_grad.1, ...), custom_call_target="tpu_custom_call" | custom-call | flops 11274289152 | bytes 22020096 | tf_op jit(solution)/shard_map/pallas_call | solution.py:525
  153.0 1.2 slice_bitcast_fusion
  154.2 0.0 copy-start
  154.2 0.0 copy-start.3
  154.2 12.1 %bitcast_multiply_fusion.2 = f32[896,4096]{1,0:T(8,128)} fusion(bf16[2,256,896]{2,1,0:T(8,128)(2,1)} %get-tuple-element.13, bf16[2,256,4096]{2,1,0:T(8,128)(2,1)} %get-tuple-element.14), kind=kOutput, calls=%fused_computation.2 | convolution fusion | flops 3761766400 | bytes 19791872 | tf_op jit(solution)/shard_map/tf,td->fd/dot_general | solution.py:596
  166.3 0.0 copy-done
  166.3 0.0 copy-done.3
  166.3 0.0 copy-start.1
  166.3 0.0 copy-start.2
  166.3 7.6 %bitcast_multiply_fusion.1 = f32[896,4096]{1,0:T(8,128)} fusion(bf16[2,256,896]{2,1,0:T(8,128)(2,1)S(1)} %copy-done.3, bf16[2,256,4096]{2,1,0:T(8,128)(2,1)S(1)} %copy-done), kind=kOutput, calls=%fused_computation.1 | convolution fusion | flops 3761766400 | bytes 19791872 | tf_op jit(solution)/shard_map/tf,td->fd/dot_general | solution.py:596
  173.9 0.0 copy-done.1
  173.9 0.0 copy-done.2
  173.9 0.0 copy-start.4
  173.9 7.6 %bitcast_multiply_fusion = f32[896,4096]{1,0:T(8,128)} fusion(bf16[2,256,896]{2,1,0:T(8,128)(2,1)S(1)} %copy-done.2, bf16[2,256,4096]{2,1,0:T(8,128)(2,1)S(1)} %copy-done.1), kind=kOutput, calls=%fused_computation | convolution fusion | flops 3761766400 | bytes 19791872 | tf_op jit(solution)/shard_map/tf,td->fd/dot_general | solution.py:596
  181.5 0.0 copy-done.4
  181.5 0.8 copy.19
Async XLA Ops:
  154.2 12.1 %copy-start = (bf16[2,256,4096]{2,1,0:T(8,128)(2,1)S(1)}, bf16[2,256,4096]{2,1,0:T(8,128)(2,1)}, u32[]{:S(2)}) copy-start(bf16[2,256,4096]{2,1,0:T(8,128)(2,1)} %get-tuple-element.14) | copy-start | bytes 12582916
  154.2 12.1 %copy-start.3 = (bf16[2,256,896]{2,1,0:T(8,128)(2,1)S(1)}, bf16[2,256,896]{2,1,0:T(8,128)(2,1)}, u32[]{:S(2)}) copy-start(bf16[2,256,896]{2,1,0:T(8,128)(2,1)} %get-tuple-element.15) | copy-start | bytes 2752516
  166.3 7.6 %copy-start.1 = (bf16[2,256,4096]{2,1,0:T(8,128)(2,1)S(1)}, bf16[2,256,4096]{2,1,0:T(8,128)(2,1)}, u32[]{:S(2)}) copy-start(bf16[2,256,4096]{2,1,0:T(8,128)(2,1)} %get-tuple-element.17) | copy-start | bytes 12582916
  166.3 7.6 %copy-start.2 = (bf16[2,256,896]{2,1,0:T(8,128)(2,1)S(1)}, bf16[2,256,896]{2,1,0:T(8,128)(2,1)}, u32[]{:S(2)}) copy-start(bf16[2,256,896]{2,1,0:T(8,128)(2,1)} %get-tuple-element.16) | copy-start | bytes 2752516
  173.9 7.6 %copy-start.4 = (f32[128,1024]{1,0:T(8,128)S(1)}, f32[128,1024]{1,0:T(8,128)}, u32[]{:S(2)}) copy-start(f32[128,1024]{1,0:T(8,128)} %get-tuple-element.26) | copy-start | bytes 1572868
